TPU v7x, 32 devices: a whole 2x2x4 slice. The times are simulated.
32 devices in a mesh: replica: 2 (over x), expert: 16 (over z, y, core).
Axes of the slice: x: 2, y: 2, z: 4, core: 2. Of those that a mesh axis runs over, the one named last changes fastest.
Arguments:
- tokens: bfloat16 [4096, 2048], P(('replica', 'expert')), parts along dimension 0, may hold values from -6 to 6
- expert_ids: int32 [4096, 8], P(('replica', 'expert')), parts along dimension 0, may hold values from 0 to 31, all different within a row; in each aligned block of 128 rows (0 to 127, 128 to 255, ...) at most 64 rows name the same one
- gate_levels: int32 [4096, 8], P(('replica', 'expert')), parts along dimension 0, may hold values from 1 to 255
- gate_up: bfloat16 [32, 2048, 1536], P('expert'), may hold values from -0.125 to 0.125
- down_proj: bfloat16 [32, 768, 2048], P('expert'), may hold values from -0.21875 to 0.21875
Outputs:
- mixed: bfloat16 [4096, 2048], P(('replica', 'expert')), parts along dimension 0
There are 2 independent parts, one for each index of `replica`. A program takes and returns all parts, laid end to end along the dimension named above; an argument that names none is the same for every part. Nothing has to cross between parts.
Inputs may be any that keep to these rules, and one draw needn't show every extreme that they name: `expert_ids`: each row names 8 different experts. Among the 128 rows of one device (aligned blocks), no expert is named by more than 64 rows, and in every draw some expert is named by exactly 64 rows of some device.
All inputs are finite; a program needn't handle non-finite values.
Results may differ from a plain program's by a relative error of at most 0.0057.
Values may be sent and summed in bfloat16 or wider, within the bound.
A program may use at most 128 MiB of HBM per device.

v0:
```python
import jax
import jax.numpy as jnp
from jax import lax
from jax.sharding import PartitionSpec as P


def apply_expert(rows, weight_in, weight_out, live_rows):
    projected = jnp.dot(rows, weight_in, preferred_element_type=jnp.float32)
    half_width = weight_out.shape[0]
    hidden = jax.nn.silu(projected[:, :half_width]) * projected[:, half_width:]
    hidden = jnp.where(live_rows[:, None], hidden, 0.0)
    hidden = hidden.astype(jnp.bfloat16)
    return jnp.dot(hidden, weight_out, preferred_element_type=jnp.float32).astype(jnp.bfloat16)


def on_device(tokens, expert_ids, gate_levels, gate_up, down_proj):
    tok_dev, width = tokens.shape
    top = expert_ids.shape[1]
    sources = lax.axis_size("expert")
    exp_dev = gate_up.shape[0]
    experts = exp_dev * sources
    slot_cap = tok_dev * top * 2 // experts
    flat_experts = expert_ids.reshape(-1)
    choose = (flat_experts[:, None] == jnp.arange(experts, dtype=jnp.int32)[None, :]).astype(
        jnp.int32
    )
    before = jnp.cumsum(choose, axis=0) - choose
    slot_number = jnp.sum(before * choose, axis=1)
    place = flat_experts * slot_cap + slot_number
    owner = jnp.arange(tok_dev * top, dtype=jnp.int32) // top
    blank = jnp.zeros((1, width), jnp.bfloat16)
    filled = jnp.full((experts * slot_cap,), tok_dev, jnp.int32).at[place].set(owner)
    outgoing = jnp.concatenate([tokens, blank], axis=0)[filled].reshape(experts, slot_cap, width)
    load = jnp.sum(choose, axis=0).reshape(experts, 1)
    received, counts = (
        lax.all_to_all(outgoing, "expert", split_axis=0, concat_axis=1, tiled=True),
        lax.all_to_all(load, "expert", split_axis=0, concat_axis=1, tiled=True),
    )
    results = []
    for expert in range(exp_dev):
        slot_place = jnp.arange(sources * slot_cap, dtype=jnp.int32) % slot_cap
        live_rows = slot_place < jnp.repeat(
            counts[expert], slot_cap, total_repeat_length=sources * slot_cap
        )
        results.append(
            apply_expert(received[expert], gate_up[expert], down_proj[expert], live_rows)
        )
    returned = lax.all_to_all(jnp.stack(results), "expert", split_axis=1, concat_axis=0, tiled=True)
    picked = returned.reshape(experts * slot_cap, width)[place].reshape(tok_dev, top, width)
    weights = gate_levels.astype(jnp.float32)
    weights = weights / jnp.sum(weights, axis=1, keepdims=True)
    return jnp.sum(weights[:, :, None] * picked.astype(jnp.float32), axis=1).astype(jnp.bfloat16)


def solution(mesh):
    in_specs = (
        P(("replica", "expert"), None),
        P(("replica", "expert"), None),
        P(("replica", "expert"), None),
        P("expert", None, None),
        P("expert", None, None),
    )
    out_specs = P(("replica", "expert"), None)
    return jax.shard_map(
        on_device, mesh=mesh, in_specs=in_specs, out_specs=out_specs, check_vma=False
    )
```

profile of v0, /device:TPU:13, one launch (start us, length us, event | category | flops | bytes accessed | tf_op | source)
XLA Modules:
  0.0 500.3 jit_solution(6860227535301394191)
XLA Ops:
  0.0 0.8 copy.16
  0.8 0.1 eq.28
  0.9 0.1 eq.32
  1.0 9.0 %reduce-window.14 = s32[32,8,128]{2,1,0:T(8,128)S(1)} reduce-window(s32[32,8,128]{2,1,0:T(8,128)S(1)} %fusion.25, s32[]{:T(128)} %constant.129.clone.1), window={size=1x1x128 pad=0_0x0_0x127_0}, to_apply=%region_2.4 | reduce-window | flops 4161536 | bytes 262148 | tf_op jit(solution)/shard_map/reduce-window.3
  10.0 0.1 slice.154
  10.1 0.1 copy.20
  10.3 0.1 copy.21
  10.3 0.1 broadcast_add_fusion
  10.5 0.1 convert_reduce_fusion
  10.6 0.7 all_to_all.34
  11.3 6.6 %all-to-all-start = ((s32[16,2,1]{1,2,0:T(1,128)}), s32[16,2,1]{1,2,0:T(1,128)S(1)}, u32[]{:S(2)}, u32[]{:S(2)}) async-start(s32[16,2,1]{1,2,0:T(1,128)} %bitcast.1), calls=%async_computation | async-start | bytes 16384 | tf_op jit(solution)/shard_map/all_to_all | solution.py:37
  17.8 0.7 broadcast_multiply_fusion
  18.5 0.1 copy.18
  18.6 0.1 mul.43
  18.8 4.3 scatter_custom_fusion
  23.1 1.1 concatenate.9
  24.2 11.0 %gather_fusion = bf16[2048,2048]{1,0:T(8,128)(2,1)} fusion(bf16[129,2048]{1,0:T(8,128)(2,1)S(1)} %concatenate.9, s32[2048]{0:T(1024)S(1)} %fusion.26), kind=kCustom, calls=%fused_computation | custom fusion | bytes 16785408 | tf_op jit(solution)/shard_map/gather | solution.py:33
  35.2 0.0 all-to-all-done
  35.2 0.0 copy-start
  35.2 6.2 %all-to-all-start.1 = ((bf16[32,64,2048]{2,1,0:T(8,128)(2,1)}), bf16[32,64,2048]{2,1,0:T(8,128)(2,1)}, u32[]{:S(2)}, u32[]{:S(2)}) async-start(bf16[32,64,2048]{2,1,0:T(8,128)(2,1)} %bitcast.182), calls=%async_computation.1 | async-start | bytes 16777216 | tf_op jit(solution)/shard_map/all_to_all | solution.py:36
  41.4 0.7 slice_reduce_fusion.1
  42.1 0.7 fusion.59
  42.8 0.7 fusion.58
  43.5 0.0 copy-done
  43.5 10.0 %select_compare_fusion = pred[1024]{0:T(1024)(128)(4,1)S(1)} fusion(s32[]{:T(128)} %bitcast.45, s32[]{:T(128)} %bitcast.44, s32[]{:T(128)} %bitcast.43, s32[]{:T(128)} %bitcast.42, s32[]{:T(128)} %bitcast.41, s32[]{:T(128)} %bitcast.40, s32[]{:T(128)} %bitcast.39, s32[]{:T(128)} %bitcast.38, s32[]{:T(128)} %bitcast.37, s32[]{:T(128)} %bitcast.36, ...), kind=kLoop, calls=%fused_computation.52 | loop fusion | flops 47104 | bytes 5216 | tf_op jit(solution)/shard_map/lt | solution.py:42
  53.6 10.0 %select_compare_fusion.1 = pred[1024]{0:T(1024)(128)(4,1)S(1)} fusion(s32[]{:T(128)} %bitcast.18, s32[]{:T(128)} %bitcast.17, s32[]{:T(128)} %bitcast.16, s32[]{:T(128)} %bitcast.15, s32[]{:T(128)} %bitcast.14, s32[]{:T(128)} %bitcast.13, s32[]{:T(128)} %bitcast.12, s32[]{:T(128)} %bitcast.11, s32[]{:T(128)} %bitcast.10, s32[]{:T(128)} %bitcast.9, ...), kind=kLoop, calls=%fused_computation.53 | loop fusion | flops 47104 | bytes 5216 | tf_op jit(solution)/shard_map/lt | solution.py:42
  63.6 160.2 %all-to-all-done.1 = bf16[32,64,2048]{2,1,0:T(8,128)(2,1)} async-done(((bf16[32,64,2048]{2,1,0:T(8,128)(2,1)}), bf16[32,64,2048]{2,1,0:T(8,128)(2,1)}, u32[]{:S(2)}, u32[]{:S(2)}) %all-to-all-start.1) | async-done | bytes 8388640 | tf_op jit(solution)/shard_map/all_to_all | solution.py:36
  223.7 0.0 slice-start
  223.7 4.1 fusion.57
  227.9 0.0 slice-start.1
  227.9 0.0 slice-start.2
  227.9 0.0 slice-start.3
  227.9 10.6 %fusion.1 = f32[1024,1536]{1,0:T(8,128)} fusion(bf16[1024,2048]{1,0:T(8,128)(2,1)S(1)} %bitcast.184, bf16[2,2048,1536]{2,1,0:T(8,128)(2,1)} %param.14), kind=kOutput, calls=%fused_computation.6 | convolution fusion | flops 6442450944 | bytes 16777216 | tf_op jit(solution)/shard_map/dot_general | solution.py:8
  238.5 0.0 slice-start.4
  238.5 0.0 slice-done
  238.5 0.0 slice-done.1
  238.5 0.0 slice-done.2
  238.5 8.7 %fusion.3 = f32[1024,1536]{1,0:T(8,128)} fusion(bf16[1024,2048]{1,0:T(8,128)(2,1)S(1)} %bitcast.183, bf16[2,2048,1536]{2,1,0:T(8,128)(2,1)S(1)} %bitcast.192), kind=kOutput, calls=%fused_computation.8 | convolution fusion | flops 6442450944 | bytes 16777216 | tf_op jit(solution)/shard_map/dot_general | solution.py:8
  247.2 0.0 slice-done.3
  247.2 0.0 slice-done.4
  247.2 0.0 copy-start.2
  247.2 6.5 %convert_bitcast_fusion = bf16[1,1024,2048]{2,1,0:T(8,128)(2,1)S(1)} fusion(bf16[2,768,2048]{2,1,0:T(8,128)(2,1)S(1)} %bitcast.194, f32[1024,1536]{1,0:T(8,128)} %fusion.1, pred[1024]{0:T(1024)(128)(4,1)S(1)} %select_compare_fusion), kind=kOutput, calls=%fused_computation.12 | convolution fusion | flops 3228827648 | bytes 13632512 | tf_op jit(solution)/shard_map/dot_general | solution.py:13
  253.7 0.0 copy-done.2
  253.7 5.4 %convert_bitcast_fusion.1 = bf16[1,1024,2048]{2,1,0:T(8,128)(2,1)} fusion(bf16[2,768,2048]{2,1,0:T(8,128)(2,1)S(1)} %bitcast.194, f32[1024,1536]{1,0:T(8,128)S(1)} %copy-done.2, pred[1024]{0:T(1024)(128)(4,1)S(1)} %select_compare_fusion.1), kind=kOutput, calls=%fused_computation.13 | convolution fusion | flops 3228827648 | bytes 13632512 | tf_op jit(solution)/shard_map/dot_general | solution.py:13
  259.2 6.2 %pad_maximum_fusion = bf16[2,1024,2048]{2,1,0:T(8,128)(2,1)} fusion(bf16[1,1024,2048]{2,1,0:T(8,128)(2,1)S(1)} %convert_bitcast_fusion, bf16[1,1024,2048]{2,1,0:T(8,128)(2,1)} %convert_bitcast_fusion.1), kind=kLoop, calls=%fused_computation.3 | loop fusion | flops 4194304 | bytes 16777216 | tf_op jit(solution)/shard_map/stack | solution.py:48
  265.3 16.4 %copy.22 = bf16[2,1024,2048]{2,0,1:T(2,128)(2,1)} copy(bf16[2,1024,2048]{2,1,0:T(8,128)(2,1)} %pad_maximum_fusion) | data formatting | bytes 16777216 | tf_op jit(solution)/shard_map/stack | solution.py:48
  281.7 0.0 copy-start.1
  281.7 5.1 %all-to-all-start.2 = ((bf16[2,1024,2048]{2,0,1:T(2,128)(2,1)}), bf16[2,1024,2048]{2,0,1:T(2,128)(2,1)}, u32[]{:S(2)}, u32[]{:S(2)}) async-start(bf16[2,1024,2048]{2,0,1:T(2,128)(2,1)} %copy.22), calls=%async_computation.2 | async-start | bytes 16777216 | tf_op jit(solution)/shard_map/all_to_all | solution.py:48
  286.8 0.0 copy-done.1
  286.8 0.1 copy.15
  286.9 182.2 %all-to-all-done.2 = bf16[2,1024,2048]{2,0,1:T(2,128)(2,1)} async-done(((bf16[2,1024,2048]{2,0,1:T(2,128)(2,1)}), bf16[2,1024,2048]{2,0,1:T(2,128)(2,1)}, u32[]{:S(2)}, u32[]{:S(2)}) %all-to-all-start.2) | async-done | bytes 8388640 | tf_op jit(solution)/shard_map/all_to_all | solution.py:48
  469.1 10.5 %copy.23 = bf16[2,16,64,2048]{3,2,0,1:T(8,128)(2,1)} copy(bf16[2,16,64,2048]{3,0,2,1:T(2,128)(2,1)} %bitcast.51) | data formatting | bytes 16777216 | tf_op jit(solution)/shard_map/all_to_all | solution.py:48
  479.7 13.3 %gather_fusion.1 = bf16[1024,2048]{1,0:T(8,128)(2,1)} fusion(bf16[2048,2048]{1,0:T(8,128)(2,1)} %bitcast.181, s32[1024]{0:T(1024)S(1)} %broadcast_clamp_fusion), kind=kCustom, calls=%fused_computation.1 | custom fusion | bytes 8392704 | tf_op jit(solution)/shard_map/gather | solution.py:49
  493.0 7.3 %fusion = bf16[128,2048]{1,0:T(8,128)(2,1)} fusion(bf16[1024,2048]{1,0:T(8,128)(2,1)} %gather_fusion.1, f32[128,8]{1,0:T(8,128)S(1)} %copy.15), kind=kLoop, calls=%fused_computation.5 | loop fusion | flops 6029312 | bytes 4722688 | tf_op jit(solution)/shard_map/reduce_sum | solution.py:52
  (12 shorter events, 0.1 us)
Async XLA Ops:
  11.3 23.9 %all-to-all-start = ((s32[16,2,1]{1,2,0:T(1,128)}), s32[16,2,1]{1,2,0:T(1,128)S(1)}, u32[]{:S(2)}, u32[]{:S(2)}) async-start(s32[16,2,1]{1,2,0:T(1,128)} %bitcast.1), calls=%async_computation | async-start | bytes 16384 | tf_op jit(solution)/shard_map/all_to_all | solution.py:37
  35.2 8.3 %copy-start = (s32[8,128]{1,0:T(8,128)S(1)}, s32[8,128]{1,0:T(8,128)}, u32[]{:S(2)}) copy-start(s32[8,128]{1,0:T(8,128)} %constant.132.clone.1) | copy-start | bytes 12292
  35.2 188.5 %all-to-all-start.1 = ((bf16[32,64,2048]{2,1,0:T(8,128)(2,1)}), bf16[32,64,2048]{2,1,0:T(8,128)(2,1)}, u32[]{:S(2)}, u32[]{:S(2)}) async-start(bf16[32,64,2048]{2,1,0:T(8,128)(2,1)} %bitcast.182), calls=%async_computation.1 | async-start | bytes 16777216 | tf_op jit(solution)/shard_map/all_to_all | solution.py:36
  223.7 14.8 %slice-start = ((s8[12582912]{0:T(1024)(128)(4,1)}), s8[4194304]{0:T(1024)(128)(4,1)S(1)}, s32[]{:S(2)}) async-start(s8[12582912]{0:T(1024)(128)(4,1)} %bitcast.191), calls=%async_computation.3 | async-start | bytes 8388608
  227.9 10.6 %slice-start.1 = ((s8[12582912]{0:T(1024)(128)(4,1)}), s8[4194304]{0:T(1024)(128)(4,1)S(1)}, s32[]{:S(2)}) async-start(s8[12582912]{0:T(1024)(128)(4,1)} %bitcast.191), calls=%async_computation.4 | async-start | bytes 8388608
  227.9 10.6 %slice-start.2 = ((s8[12582912]{0:T(1024)(128)(4,1)}), s8[4194304]{0:T(1024)(128)(4,1)S(1)}, s32[]{:S(2)}) async-start(s8[12582912]{0:T(1024)(128)(4,1)} %bitcast.191), calls=%async_computation.5 | async-start | bytes 8388608
  227.9 19.3 %slice-start.3 = ((s8[6291456]{0:T(1024)(128)(4,1)}), s8[4194304]{0:T(1024)(128)(4,1)S(1)}, s32[]{:S(2)}) async-start(s8[6291456]{0:T(1024)(128)(4,1)} %bitcast.193), calls=%async_computation.6 | async-start | bytes 8388608
  238.5 8.7 %slice-start.4 = ((s8[6291456]{0:T(1024)(128)(4,1)}), s8[2097152]{0:T(1024)(128)(4,1)S(1)}, s32[]{:S(2)}) async-start(s8[6291456]{0:T(1024)(128)(4,1)} %bitcast.193), calls=%async_computation.7 | async-start | bytes 4194304
  247.2 6.5 %copy-start.2 = (f32[1024,1536]{1,0:T(8,128)S(1)}, f32[1024,1536]{1,0:T(8,128)}, u32[]{:S(2)}) copy-start(f32[1024,1536]{1,0:T(8,128)} %fusion.3) | copy-start | bytes 18874372
  281.7 5.1 %copy-start.1 = (s32[128,8]{0,1:T(8,128)S(1)}, s32[128,8]{0,1:T(8,128)}, u32[]{:S(2)}) copy-start(s32[128,8]{0,1:T(8,128)} %param.13) | copy-start | bytes 12292
  281.7 187.4 %all-to-all-start.2 = ((bf16[2,1024,2048]{2,0,1:T(2,128)(2,1)}), bf16[2,1024,2048]{2,0,1:T(2,128)(2,1)}, u32[]{:S(2)}, u32[]{:S(2)}) async-start(bf16[2,1024,2048]{2,0,1:T(2,128)(2,1)} %copy.22), calls=%async_computation.2 | async-start | bytes 16777216 | tf_op jit(solution)/shard_map/all_to_all | solution.py:48
where the time goes:
time: 501 us; the launch traced here: 500 us
  waiting for transfers between devices  342 us (68%)
  local copies, waits for them, and re-layouts  65.2 us (13%)
  other arithmetic  43.6 us (9%)
  matrix products  31.2 us (6%)
  starting transfers between devices  17.8 us (4%)
    all_to_all x1, waiting for transfers between devices, on_device(): lax.all_to_all(jnp.stack(results), 'expert', split_axis=1, concat_axis=0,...  182 us
    all_to_all x1, waiting for transfers between devices, on_device(): lax.all_to_all(outgoing, 'expert', split_axis=0, concat_axis=1, tiled=True)  160 us
    lt x2, other arithmetic, on_device(): slot_place < jnp.repeat(counts[expert], slot_cap, total_repeat_length=sou...  20 us
    dot_general x2, matrix products, apply_expert(): projected = jnp.dot(rows, weight_in, preferred_element_type=jnp.float32)  19.3 us
    another operation x1, local copies, waits for them, and re-layouts, on_device(): jnp.stack(results)  16.4 us
    gather x1, local copies, waits for them, and re-layouts, on_device(): returned.reshape(experts * slot_cap, width)[place]  13.3 us
    dot_general x2, matrix products, apply_expert(): jnp.dot(hidden, weight_out, preferred_element_type=jnp.float32)  11.9 us
    gather x1, local copies, waits for them, and re-layouts, on_device(): jnp.concatenate([tokens, blank], axis=0)[filled]  11 us
  transfers between devices with their start and end apart: 3, of which 2 were waited for; matrix products, arithmetic and copies ran while one was open for 8% of the time, Pallas kernels for 0%

commit v1 on v0

v1 whole, which is shorter than its diff:
```python
import jax
import jax.numpy as jnp
from jax import lax
from jax.sharding import PartitionSpec as P


def on_device(tokens, expert_ids, gate_levels, gate_up, down_proj):
    exp_dev = gate_up.shape[0]
    half = down_proj.shape[1]
    weights = gate_levels.astype(jnp.float32)
    weights = weights / jnp.sum(weights, axis=1, keepdims=True)
    all_tokens = lax.all_gather(tokens, "expert", axis=0, tiled=True)
    all_ids = lax.all_gather(expert_ids, "expert", axis=0, tiled=True)
    all_weights = lax.all_gather(weights, "expert", axis=0, tiled=True)
    first = lax.axis_index("expert") * exp_dev
    parts = []
    for expert in range(exp_dev):
        named = all_ids == first + expert
        share = jnp.sum(jnp.where(named, all_weights, 0.0), axis=1, keepdims=True)
        projected = jnp.dot(all_tokens, gate_up[expert], preferred_element_type=jnp.float32)
        hidden = jax.nn.silu(projected[:, :half]) * projected[:, half:]
        parts.append((hidden * share).astype(jnp.bfloat16))
    hidden = jnp.concatenate(parts, axis=1)
    down = down_proj.reshape(exp_dev * half, down_proj.shape[2])
    partial = jnp.dot(hidden, down, preferred_element_type=jnp.float32).astype(jnp.bfloat16)
    return lax.psum_scatter(partial, "expert", scatter_dimension=0, tiled=True)


def solution(mesh):
    rows = P(("replica", "expert"), None)
    return jax.shard_map(
        on_device,
        mesh=mesh,
        in_specs=(rows, rows, rows, P("expert", None, None), P("expert", None, None)),
        out_specs=rows,
        check_vma=False,
    )
```

time: 501 us -> 260 us (0.52)
  the two profiles are of different devices: /device:TPU:13 before, /device:TPU:0 now
where the time goes in v1:
time: 260 us
  waiting for transfers between devices  141 us (54%)
  matrix products  54.9 us (21%)
  blocking collectives  41.7 us (16%)
  between operations  13.4 us (5%)
  other arithmetic  8.87 us (3%)
    reduce_scatter x1, waiting for transfers between devices, on_device(): return lax.psum_scatter(partial, 'expert', scatter_dimension=0, tiled=True)  103 us
    all_gather x1, waiting for transfers between devices, on_device(): all_tokens = lax.all_gather(tokens, 'expert', axis=0, tiled=True)  37 us
    dot_general x2, matrix products, on_device(): jnp.dot(all_tokens, gate_up[expert], preferred_element_type=jnp.float32)  36.7 us
    all_gather x1, blocking collectives, on_device(): all_weights = lax.all_gather(weights, 'expert', axis=0, tiled=True)  23.6 us
    dot_general x1, matrix products, on_device(): jnp.dot(hidden, down, preferred_element_type=jnp.float32)  18.1 us
    all_gather x1, blocking collectives, on_device(): all_ids = lax.all_gather(expert_ids, 'expert', axis=0, tiled=True)  18.1 us
    convert_element_type x1, other arithmetic, on_device(): parts.append((hidden * share).astype(jnp.bfloat16))  7.43 us
  transfers between devices with their start and end apart: 2, of which 2 were waited for; matrix products, arithmetic and copies ran while one was open for 1% of the time, Pallas kernels for 0%

profile of v1, /device:TPU:0, one launch (start us, length us, event | category | flops | bytes accessed | tf_op | source)
XLA Modules:
  0.0 259.6 jit_solution(13736908685529999688)
XLA Ops:
  6.5 0.0 all-gather.2.cloned.1.call-start
  6.5 0.7 all-gather.2.cloned.1.call-update
  7.3 0.0 reduce-scatter.2.cloned.1.call-start
  7.3 0.7 convert_reduce_fusion
  8.0 0.7 convert_divide_fusion
  8.7 23.6 %all_gather.11 = f32[2048,8]{0,1:T(8,128)S(1)} all-gather(f32[128,8]{0,1:T(8,128)S(1)} %convert_divide_fusion), channel_id=1, replica_groups=mesh['replica'=2,'expert'=16] {'expert'}, dimensions={0}, use_global_device_ids=true | all-gather | bytes 69632 | tf_op jit(solution)/shard_map/all_gather | solution.py:14
  32.3 18.1 %all_gather.10 = s32[2048,8]{0,1:T(8,128)S(1)} all-gather(s32[128,8]{0,1:T(8,128)} %param.6), channel_id=1, replica_groups=mesh['replica'=2,'expert'=16] {'expert'}, dimensions={0}, use_global_device_ids=true | all-gather | bytes 69632 | tf_op jit(solution)/shard_map/all_gather | solution.py:13
  50.5 37.0 %all-gather.2.cloned.1.call-done = bf16[2048,2048]{1,0:T(8,128)(2,1)} async-done(((bf16[128,2048]{1,0:T(8,128)(2,1)}), bf16[2048,2048]{1,0:T(8,128)(2,1)}) %all-gather.2.cloned.1.call-update) | async-done | bytes 8388624 | tf_op jit(solution)/shard_map/all_gather | solution.py:12
  87.4 17.7 %fusion.7 = f32[2048,1536]{0,1:T(8,128)S(1)} fusion(bf16[2048,2048]{1,0:T(8,128)(2,1)} %all-gather.2.cloned.1.call-done, bf16[2,2048,1536]{2,1,0:T(8,128)(2,1)} %param.8), kind=kOutput, calls=%fused_computation.10 | convolution fusion | flops 12884901888 | bytes 27262976 | tf_op jit(solution)/shard_map/dot_general | solution.py:20
  105.1 19.0 %fusion.9 = f32[2048,1536]{0,1:T(8,128)} fusion(bf16[2048,2048]{1,0:T(8,128)(2,1)} %all-gather.2.cloned.1.call-done, bf16[2,2048,1536]{2,1,0:T(8,128)(2,1)} %param.8), kind=kOutput, calls=%fused_computation.12 | convolution fusion | flops 12884901888 | bytes 27262976 | tf_op jit(solution)/shard_map/dot_general | solution.py:20
  124.1 7.4 %fusion.1 = (bf16[2048,768]{0,1:T(8,128)(2,1)S(1)}, bf16[2048,768]{0,1:T(8,128)(2,1)S(1)}) fusion(f32[2048,1536]{0,1:T(8,128)S(1)} %fusion.7, f32[2048]{0:T(1024)S(1)} %get-tuple-element.6, f32[2048]{0:T(1024)S(1)} %get-tuple-element.5, f32[2048,1536]{0,1:T(8,128)} %fusion.9), kind=kLoop, calls=%fused_computation.3 | loop fusion | flops 22020096 | bytes 31473664 | tf_op jit(solution)/shard_map/convert_element_type | solution.py:22
  131.6 18.1 %convolution_convert_fusion = bf16[2048,2048]{1,0:T(8,128)(2,1)} fusion(bf16[1536,2048]{1,0:T(8,128)(2,1)} %bitcast.10, bf16[2048,768]{0,1:T(8,128)(2,1)S(1)} %get-tuple-element.7, bf16[2048,768]{0,1:T(8,128)(2,1)S(1)} %get-tuple-element.8), kind=kOutput, calls=%fused_computation | convolution fusion | flops 12901679104 | bytes 20971520 | tf_op jit(solution)/shard_map/dot_general | solution.py:25
  149.7 0.0 reduce-scatter.2.cloned.1.call-update
  149.7 103.0 %reduce-scatter.2.cloned.1.call-done = bf16[128,2048]{1,0:T(8,128)(2,1)} async-done(((bf16[2048,2048]{1,0:T(8,128)(2,1)}), bf16[128,2048]{1,0:T(8,128)(2,1)}) %reduce-scatter.2.cloned.1.call-update) | async-done | bytes 524304 | tf_op jit(solution)/shard_map/reduce_scatter | solution.py:26
  (1 shorter events, 0.0 us)
Async XLA Ops:
  6.5 80.9 %all-gather.2.cloned.1.call-start = ((), (), s32[]{:S(2)}) async-start(), calls=%async_computation.1 | async-start | bytes 8912896 | tf_op jit(solution)/shard_map/all_gather | solution.py:12
  7.3 245.5 %reduce-scatter.2.cloned.1.call-start = ((), (), s32[]{:S(2)}) async-start(), calls=%async_computation.2 | async-start | bytes 8912896 | tf_op jit(solution)/shard_map/reduce_scatter | solution.py:26
Sparse Core Ops, SparseCore 0:
  9.5 77.8 all-gather.1
  149.9 102.8 reduce-scatter.1

commit v2 on v1

v2 whole, which is shorter than its diff:
```python
import functools
import jax
import jax.numpy as jnp
from jax import lax
from jax.sharding import PartitionSpec as P

PAD = 128
CUTS = 2


def apply_experts(packed, first, width, top, gate_up, down_proj):
    exp_dev, half = down_proj.shape[:2]
    rows = packed[:, :width]
    ids = packed[:, width : width + top].astype(jnp.int32)
    levels = packed[:, width + top : width + 2 * top].astype(jnp.float32)
    weights = levels / jnp.sum(levels, axis=1, keepdims=True)
    parts = []
    for expert in range(exp_dev):
        share = jnp.sum(jnp.where(ids == first + expert, weights, 0.0), axis=1, keepdims=True)
        projected = jnp.dot(rows, gate_up[expert], preferred_element_type=jnp.float32)
        hidden = jax.nn.silu(projected[:, :half]) * projected[:, half:]
        parts.append((hidden * share).astype(jnp.bfloat16))
    down = down_proj.reshape(exp_dev * half, width)
    return jnp.dot(
        jnp.concatenate(parts, axis=1), down, preferred_element_type=jnp.float32
    ).astype(jnp.bfloat16)


def add(*terms):
    total = terms[0].astype(jnp.float32)
    for term in terms[1:]:
        total = total + term.astype(jnp.float32)
    return total.astype(jnp.bfloat16)


def on_device(y_size, tokens, expert_ids, gate_levels, gate_up, down_proj):
    tok_dev, width = tokens.shape
    top = expert_ids.shape[1]
    n = lax.axis_size("expert")
    z_size = n // (2 * y_size)
    me = lax.axis_index("expert")
    core, y, z = me % 2, (me // 2) % y_size, me // (2 * y_size)
    first = me * gate_up.shape[0]

    packed = jnp.concatenate(
        [
            tokens,
            expert_ids.astype(jnp.bfloat16),
            gate_levels.astype(jnp.bfloat16),
            jnp.zeros((tok_dev, PAD - 2 * top), jnp.bfloat16),
        ],
        axis=1,
    )
    gathered = lax.all_gather(packed, "expert", axis=0, tiled=True)
    gathered = gathered.reshape(z_size, y_size, 2, tok_dev, width + PAD)

    def group(y_to, core_to, after):
        rows = lax.dynamic_slice(
            gathered, (0, y_to, core_to, 0, 0), (z_size, 1, 1, tok_dev, width + PAD)
        ).reshape(z_size * tok_dev, width + PAD)
        if after is not None:
            rows, after = lax.optimization_barrier((rows, after))
        part = apply_experts(rows, first, width, top, gate_up, down_proj)
        return part, after

    core_pairs = [(i, i ^ 1) for i in range(n)]
    y_pairs = [(i, i ^ 2) for i in range(n)]
    from_y = None
    last = None
    for y_to in [(y + step) % y_size for step in range(1, y_size)] + [y]:
        away, last = group(y_to, 1 - core, last)
        arrived = lax.ppermute(away, "expert", core_pairs)
        kept, _ = group(y_to, core, away)
        last = lax.optimization_barrier(kept)
        if y_to is y:
            terms = [last, arrived] + ([] if from_y is None else [from_y])
            total = add(*terms)
        else:
            from_y = lax.ppermute(add(last, arrived), "expert", y_pairs)

    total = total.reshape(z_size, tok_dev, width)
    step_z = 2 * y_size
    columns = width // CUTS
    outs = []
    for cut in range(CUTS):
        own = total[:, :, cut * columns : (cut + 1) * columns]

        def block(at):
            return lax.dynamic_index_in_dim(own, jnp.clip(at, 0, z_size - 1), 0, keepdims=False)

        up, down = None, None
        for step in range(z_size - 1):
            reach = z_size - 1 - step
            up_block, down_block = block(z + reach), block(z - reach)
            up = up_block if up is None else add(up, up_block)
            down = down_block if down is None else add(down, down_block)
            up_pairs = [(i, i + step_z) for i in range(n) if i // step_z + reach < z_size]
            down_pairs = [(i, i - step_z) for i in range(n) if i // step_z >= reach]
            up = lax.ppermute(up, "expert", up_pairs)
            down = lax.ppermute(down, "expert", down_pairs)
        outs.append(add(block(z), up, down) if z_size > 1 else own[0])
    return jnp.concatenate(outs, axis=1)


def solution(mesh):
    y_size = max(1, 4 // mesh.shape["replica"])
    rows = P(("replica", "expert"), None)
    return jax.shard_map(
        functools.partial(on_device, y_size),
        mesh=mesh,
        in_specs=(rows, rows, rows, P("expert", None, None), P("expert", None, None)),
        out_specs=rows,
        check_vma=False,
    )
```

time: 260 us -> 254 us (0.977)
  blocking collectives: 41.7 us -> 0 us
  starting transfers between devices: 0.04 us -> 32.7 us
  waiting for transfers between devices: 141 us -> 128 us
  other arithmetic: 8.87 us -> 18 us
  local copies, waits for them, and re-layouts: 0 us -> 7.09 us
    reduce_scatter x1 -> x0, waiting for transfers between devices: 103 us -> none  [on_device(): return lax.psum_scatter(partial, 'expert', scatter_dimension=0, tiled=True)]
    ppermute x0 -> x15, waiting for transfers between devices: none -> 46.7 us  [the longest x1 39.1 us: on_device(): from_y = lax.ppermute(add(last, arrived), 'expert', y_pairs)]
    all_gather x1, waiting for transfers between devices: 37 us -> 81 us  [on_device(): gathered = lax.all_gather(packed, 'expert', axis=0, tiled=True)]
    all_gather x2 -> x0, blocking collectives: 41.7 us -> none  [the longest x1 23.6 us: on_device(): all_weights = lax.all_gather(weights, 'expert', axis=0, tiled=True)]
    ppermute x0 -> x15, starting transfers between devices: none -> 32.7 us  [the longest x6 24.8 us: on_device(): up = lax.ppermute(up, 'expert', up_pairs)]
    convert_element_type x1 -> x17, other arithmetic: 7.43 us -> 15 us  [the longest x8 10 us: add(): return total.astype(jnp.bfloat16)]
    dynamic_slice x0 -> x1, local copies, waits for them, and re-layouts: none -> 4.61 us  [group(): lax.dynamic_slice(gathered, (0, y_to, core_to, 0, 0), (z_size, 1, 1, tok_...]
    dot_general x3 -> x12, matrix products: 54.9 us -> 53.5 us  [the longest x8 36.6 us: apply_experts(): jnp.dot(rows, gate_up[expert], preferred_element_type=jnp.float32)]
  transfers between devices with their start and end apart: 2 -> 16, of which waited for: 2 -> 5; matrix products, arithmetic and copies ran while one was open for 1% -> 11% of each run, Pallas kernels for 0% -> 0%
where the time goes in v2:
time: 254 us; the launch traced here: 253 us
  waiting for transfers between devices  128 us (50%)
  matrix products  53.5 us (21%)
  starting transfers between devices  32.7 us (13%)
  other arithmetic  18 us (7%)
  between operations  14 us (6%)
  local copies, waits for them, and re-layouts  7.09 us (3%)
    all_gather x1, waiting for transfers between devices, on_device(): gathered = lax.all_gather(packed, 'expert', axis=0, tiled=True)  81 us
    ppermute x1, waiting for transfers between devices, on_device(): from_y = lax.ppermute(add(last, arrived), 'expert', y_pairs)  39.1 us
    dot_general x8, matrix products, apply_experts(): jnp.dot(rows, gate_up[expert], preferred_element_type=jnp.float32)  36.6 us
    ppermute x6, starting transfers between devices, on_device(): up = lax.ppermute(up, 'expert', up_pairs)  24.8 us
    dot_general x4, matrix products, apply_experts(): jnp.dot(jnp.concatenate(parts, axis=1), down, preferred_element_type=jnp....  16.9 us
    convert_element_type x8, other arithmetic, add(): return total.astype(jnp.bfloat16)  10 us
    ppermute x6, starting transfers between devices, on_device(): down = lax.ppermute(down, 'expert', down_pairs)  6.7 us
    ppermute x6, waiting for transfers between devices, on_device(): down = lax.ppermute(down, 'expert', down_pairs)  5.87 us
  transfers between devices with their start and end apart: 16, of which 5 were waited for; matrix products, arithmetic and copies ran while one was open for 11% of the time, Pallas kernels for 0%

profile of v2, /device:TPU:0, one launch (start us, length us, event | category | flops | bytes accessed | tf_op | source)
XLA Modules:
  0.0 253.0 jit_solution(16927647212984138359)
XLA Ops:
  6.5 0.7 convert_element_type.213
  7.2 0.1 copy.6
  7.4 0.7 convert_element_type.214
  8.0 0.1 copy.7
  8.2 1.9 concatenate.18
  10.0 0.0 all-gather.2.cloned.1.call-update
  10.1 81.0 %all-gather.2.cloned.1.call-done = bf16[2048,2176]{1,0:T(8,128)(2,1)} async-done(((bf16[128,2176]{1,0:T(8,128)(2,1)}), bf16[2048,2176]{1,0:T(8,128)(2,1)}) %all-gather.2.cloned.1.call-update) | async-done | bytes 8912912 | tf_op jit(solution)/shard_map/all_gather | solution.py:54
  91.1 4.6 %constant_dynamic-slice_fusion.3 = (bf16[4,1,1,128,2176]{4,3,2,1,0:T(8,128)(2,1)S(1)}, bf16[4,1,1,128,2176]{4,3,2,1,0:T(8,128)(2,1)S(1)}, bf16[4,1,1,128,2176]{4...) fusion(bf16[4,2,2,128,2176]{4,3,2,1,0:T(8,128)(2,1)} %bitcast.67, s32[]{:T(128)S(6)} %select_n.80, s32[]{:T(128)S(6)} %select_n.82, ...), kind=kLoop, calls=%fused_computation.128 | loop fusion | bytes 17825808 | tf_op jit(solution)/shard_map/dynamic_slice | solution.py:58
  95.7 0.2 convert_reduce_fusion.3
  96.0 5.7 %fusion.14 = f32[512,1536]{1,0:T(8,128)S(1)} fusion(bf16[2,2048,1536]{2,1,0:T(8,128)(2,1)} %param.8, bf16[512,2176]{1,0:T(8,128)(2,1)S(1)} %bitcast.82), kind=kOutput, calls=%fused_computation.14 | convolution fusion | flops 3221225472 | bytes 11534336 | tf_op jit(solution)/shard_map/dot_general | solution.py:20
  101.7 5.7 %fusion.6 = f32[512,1536]{1,0:T(8,128)S(1)} fusion(bf16[2,2048,1536]{2,1,0:T(8,128)(2,1)} %param.8, bf16[512,2176]{1,0:T(8,128)(2,1)S(1)} %bitcast.83), kind=kOutput, calls=%fused_computation.6 | convolution fusion | flops 3221225472 | bytes 11534336 | tf_op jit(solution)/shard_map/dot_general | solution.py:20
  107.4 0.3 select_reduce_fusion.7
  107.7 0.9 fusion.45
  108.6 4.7 %convolution_convert_fusion.3 = bf16[512,2048]{1,0:T(8,128)(2,1)} fusion(bf16[1536,2048]{1,0:T(8,128)(2,1)S(1)} %bitcast.91, bf16[512,768]{1,0:T(8,128)(2,1)S(1)} %get-tuple-element.37, bf16[512,768]{1,0:T(8,128)(2,1)S(1)} %get-tuple-element.38), kind=kOutput, calls=%fused_computation.29 | convolution fusion | flops 3225419776 | bytes 9961472 | tf_op jit(solution)/shard_map/dot_general | solution.py:24
  113.3 0.2 convert_reduce_fusion.2
  113.5 3.4 %fusion.12 = f32[512,1536]{1,0:T(8,128)S(1)} fusion(bf16[2,2048,1536]{2,1,0:T(8,128)(2,1)S(1)} %bitcast.86, bf16[512,2176]{1,0:T(8,128)(2,1)S(1)} %bitcast.78), kind=kOutput, calls=%fused_computation.12 | convolution fusion | flops 3221225472 | bytes 11534336 | tf_op jit(solution)/shard_map/dot_general | solution.py:20
  117.0 3.4 %fusion.4 = f32[512,1536]{1,0:T(8,128)S(1)} fusion(bf16[2,2048,1536]{2,1,0:T(8,128)(2,1)S(1)} %bitcast.86, bf16[512,2176]{1,0:T(8,128)(2,1)S(1)} %bitcast.79), kind=kOutput, calls=%fused_computation.4 | convolution fusion | flops 3221225472 | bytes 11534336 | tf_op jit(solution)/shard_map/dot_general | solution.py:20
  120.4 0.3 select_reduce_fusion.5
  120.8 0.4 fusion.43
  121.2 0.4 fusion.41
  121.7 3.7 %convolution_convert_fusion.2 = bf16[512,2048]{1,0:T(8,128)(2,1)S(1)} fusion(bf16[1536,2048]{1,0:T(8,128)(2,1)S(1)} %bitcast.92, bf16[512,768]{1,0:T(8,128)(2,1)S(1)} %fusion.41, bf16[512,768]{1,0:T(8,128)(2,1)S(1)} %fusion.43), kind=kOutput, calls=%fused_computation.28 | convolution fusion | flops 3225419776 | bytes 9961472 | tf_op jit(solution)/shard_map/dot_general | solution.py:24
  125.4 0.2 convert_reduce_fusion.1
  125.6 5.9 %fusion.10 = f32[512,1536]{1,0:T(8,128)S(1)} fusion(bf16[2,2048,1536]{2,1,0:T(8,128)(2,1)} %param.8, bf16[512,2176]{1,0:T(8,128)(2,1)S(1)} %bitcast.74), kind=kOutput, calls=%fused_computation.10 | convolution fusion | flops 3221225472 | bytes 11534336 | tf_op jit(solution)/shard_map/dot_general | solution.py:20
  131.5 5.7 %fusion.2 = f32[512,1536]{1,0:T(8,128)S(1)} fusion(bf16[2,2048,1536]{2,1,0:T(8,128)(2,1)} %param.8, bf16[512,2176]{1,0:T(8,128)(2,1)S(1)} %bitcast.75), kind=kOutput, calls=%fused_computation.2 | convolution fusion | flops 3221225472 | bytes 11534336 | tf_op jit(solution)/shard_map/dot_general | solution.py:20
  137.2 0.3 collective-permute-start.1
  137.5 0.3 select_reduce_fusion.3
  137.9 0.4 fusion.39
  138.3 0.4 fusion.37
  138.8 4.7 %convolution_convert_fusion.1 = bf16[512,2048]{1,0:T(8,128)(2,1)} fusion(bf16[1536,2048]{1,0:T(8,128)(2,1)S(1)} %bitcast.95, bf16[512,768]{1,0:T(8,128)(2,1)S(1)} %fusion.37, bf16[512,768]{1,0:T(8,128)(2,1)S(1)} %fusion.39), kind=kOutput, calls=%fused_computation.27 | convolution fusion | flops 3225419776 | bytes 9961472 | tf_op jit(solution)/shard_map/dot_general | solution.py:24
  143.5 0.2 collective-permute-start
  143.8 0.2 convert_reduce_fusion
  144.0 0.4 select_reduce_fusion.1
  144.4 3.4 %fusion.8 = f32[512,1536]{1,0:T(8,128)S(1)} fusion(bf16[2,2048,1536]{2,1,0:T(8,128)(2,1)S(1)} %bitcast.88, bf16[512,2176]{1,0:T(8,128)(2,1)S(1)} %bitcast.71), kind=kOutput, calls=%fused_computation.8 | convolution fusion | flops 3221225472 | bytes 11534336 | tf_op jit(solution)/shard_map/dot_general | solution.py:20
  147.8 0.9 add_convert_fusion.1
  148.7 0.6 collective-permute-start.2
  149.3 0.5 fusion.35
  149.8 3.4 %fusion = f32[512,1536]{1,0:T(8,128)S(1)} fusion(bf16[2,2048,1536]{2,1,0:T(8,128)(2,1)S(1)} %bitcast.88, bf16[512,2176]{1,0:T(8,128)(2,1)S(1)} %bitcast.72), kind=kOutput, calls=%fused_computation | convolution fusion | flops 3221225472 | bytes 11534336 | tf_op jit(solution)/shard_map/dot_general | solution.py:20
  153.2 0.4 fusion.33
  153.6 3.8 %convolution_convert_fusion = bf16[512,2048]{1,0:T(8,128)(2,1)S(1)} fusion(bf16[1536,2048]{1,0:T(8,128)(2,1)S(1)} %bitcast.96, bf16[512,768]{1,0:T(8,128)(2,1)S(1)} %fusion.33, bf16[512,768]{1,0:T(8,128)(2,1)S(1)} %fusion.35), kind=kOutput, calls=%fused_computation.26 | convolution fusion | flops 3225419776 | bytes 9961472 | tf_op jit(solution)/shard_map/dot_general | solution.py:24
  157.5 39.1 %collective-permute-done.2 = bf16[512,2048]{1,0:T(8,128)(2,1)S(1)} collective-permute-done((bf16[512,2048]{1,0:T(8,128)(2,1)S(1)}, bf16[512,2048]{1,0:T(8,128)(2,1)S(1)}, u32[]{:S(2)}, u32[]{:S(2)}) %collective-permute-start.2) | collective-permute-done | bytes 2097184 | tf_op jit(solution)/shard_map/ppermute | solution.py:79
  196.6 1.4 add_convert_fusion
  198.0 0.2 fusion.76
  198.3 3.3 %collective-permute-start.3 = (bf16[128,1024]{1,0:T(8,128)(2,1)S(1)}, bf16[128,1024]{1,0:T(8,128)(2,1)}, u32[]{:S(2)}, u32[]{:S(2)}) collective-permute-start(bf16[128,1024]{1,0:T(8,128)(2,1)S(1)} %get-tuple-element.29), channel_id=1, source_target_pairs={{0,4},{1,5},{2,6},{3,7},{16,20},{17,21},{18,22},{19,23}} | collective-permute-start | bytes 786440 | tf_op jit(solution)/shard_map/ppermute | solution.py:99
  201.6 1.4 collective-permute-start.6
  203.0 0.7 collective-permute-start.12
  203.7 2.0 collective-permute-start.9
  205.7 1.8 collective-permute-done.3
  207.5 1.9 fusion.69
  209.4 4.5 %collective-permute-start.4 = (bf16[128,1024]{1,0:T(8,128)(2,1)}, bf16[128,1024]{1,0:T(8,128)(2,1)S(1)}, u32[]{:S(2)}, u32[]{:S(2)}) collective-permute-start(bf16[128,1024]{1,0:T(8,128)(2,1)} %get-tuple-element.27), channel_id=1, source_target_pairs={{0,4},{1,5},{2,6},{3,7},{4,8},{5,9},{6,10},{7,11},{16,20},{17,21},... | collective-permute-start | bytes 786440 | tf_op jit(solution)/shard_map/ppermute | solution.py:99
  213.9 1.4 collective-permute-start.7
  215.3 1.8 fusion.63
  217.2 4.7 %collective-permute-start.10 = (bf16[128,1024]{1,0:T(8,128)(2,1)}, bf16[128,1024]{1,0:T(8,128)(2,1)S(1)}, u32[]{:S(2)}, u32[]{:S(2)}) collective-permute-start(bf16[128,1024]{1,0:T(8,128)(2,1)} %get-tuple-element.33), channel_id=1, source_target_pairs={{0,4},{1,5},{2,6},{3,7},{4,8},{5,9},{6,10},{7,11},{16,20},{17,21},... | collective-permute-start | bytes 786440 | tf_op jit(solution)/shard_map/ppermute | solution.py:99
  221.8 0.7 collective-permute-start.13
  222.6 1.8 fusion.68
  224.4 5.2 %collective-permute-start.5 = (bf16[128,1024]{1,0:T(8,128)(2,1)}, bf16[128,1024]{1,0:T(8,128)(2,1)S(1)}, u32[]{:S(2)}, u32[]{:S(2)}) collective-permute-start(bf16[128,1024]{1,0:T(8,128)(2,1)} %get-tuple-element.25), channel_id=1, source_target_pairs={{0,4},{1,5},{2,6},{3,7},{4,8},{5,9},{6,10},{7,11},{8,12},{9,13},{1... | collective-permute-start | bytes 786440 | tf_op jit(solution)/shard_map/ppermute | solution.py:99
  229.6 1.3 collective-permute-start.8
  230.9 0.9 fusion.62
  231.8 5.2 %collective-permute-start.11 = (bf16[128,1024]{1,0:T(8,128)(2,1)}, bf16[128,1024]{1,0:T(8,128)(2,1)S(1)}, u32[]{:S(2)}, u32[]{:S(2)}) collective-permute-start(bf16[128,1024]{1,0:T(8,128)(2,1)} %get-tuple-element.31), channel_id=1, source_target_pairs={{0,4},{1,5},{2,6},{3,7},{4,8},{5,9},{6,10},{7,11},{8,12},{9,13},{1... | collective-permute-start | bytes 786440 | tf_op jit(solution)/shard_map/ppermute | solution.py:99
  237.0 1.3 collective-permute-start.14
  238.3 2.0 collective-permute-done.8
  240.3 1.1 fusion.71
  241.4 3.9 %collective-permute-done.14 = bf16[128,1024]{1,0:T(8,128)(2,1)S(1)} collective-permute-done((bf16[128,1024]{1,0:T(8,128)(2,1)S(1)}, bf16[128,1024]{1,0:T(8,128)(2,1)S(1)}, u32[]{:S(2)}, u32[]{:S(2)}) %collective-permute-start.14) | collective-permute-done | bytes 262176 | tf_op jit(solution)/shard_map/ppermute | solution.py:100
  245.2 0.1 fusion.65
  245.4 0.8 pad_maximum_fusion
  (39 shorter events, 0.2 us)
Async XLA Ops:
  6.5 84.6 %all-gather.2.cloned.1.call-start = ((), (), s32[]{:S(2)}) async-start(), calls=%async_computation | async-start | bytes 9469952 | tf_op jit(solution)/shard_map/all_gather | solution.py:54
  95.9 12.7 %slice-start.6 = ((s8[6291456]{0:T(1024)(128)(4,1)}), s8[4194304]{0:T(1024)(128)(4,1)S(1)}, s32[]{:S(2)}) async-start(s8[6291456]{0:T(1024)(128)(4,1)} %bitcast.89), calls=%async_computation.7 | async-start | bytes 8388608
  101.7 7.0 %slice-start.7 = ((s8[6291456]{0:T(1024)(128)(4,1)}), s8[2097152]{0:T(1024)(128)(4,1)S(1)}, s32[]{:S(2)}) async-start(s8[6291456]{0:T(1024)(128)(4,1)} %bitcast.89), calls=%async_computation.8 | async-start | bytes 4194304
  107.7 5.8 %slice-start = ((s8[12582912]{0:T(1024)(128)(4,1)}), s8[4194304]{0:T(1024)(128)(4,1)S(1)}, s32[]{:S(2)}) async-start(s8[12582912]{0:T(1024)(128)(4,1)} %bitcast.85), calls=%async_computation.1 | async-start | bytes 8388608
  108.6 4.9 %slice-start.1 = ((s8[12582912]{0:T(1024)(128)(4,1)}), s8[4194304]{0:T(1024)(128)(4,1)S(1)}, s32[]{:S(2)}) async-start(s8[12582912]{0:T(1024)(128)(4,1)} %bitcast.85), calls=%async_computation.2 | async-start | bytes 8388608
  108.6 4.9 %slice-start.2 = ((s8[12582912]{0:T(1024)(128)(4,1)}), s8[4194304]{0:T(1024)(128)(4,1)S(1)}, s32[]{:S(2)}) async-start(s8[12582912]{0:T(1024)(128)(4,1)} %bitcast.85), calls=%async_computation.3 | async-start | bytes 8388608
  125.6 13.2 %slice-start.8 = ((s8[6291456]{0:T(1024)(128)(4,1)}), s8[4194304]{0:T(1024)(128)(4,1)S(1)}, s32[]{:S(2)}) async-start(s8[6291456]{0:T(1024)(128)(4,1)} %bitcast.93), calls=%async_computation.9 | async-start | bytes 8388608
  131.5 7.3 %slice-start.9 = ((s8[6291456]{0:T(1024)(128)(4,1)}), s8[2097152]{0:T(1024)(128)(4,1)S(1)}, s32[]{:S(2)}) async-start(s8[6291456]{0:T(1024)(128)(4,1)} %bitcast.93), calls=%async_computation.10 | async-start | bytes 4194304
  137.2 10.6 %collective-permute-start.1 = (bf16[512,2048]{1,0:T(8,128)(2,1)}, bf16[512,2048]{1,0:T(8,128)(2,1)S(1)}, u32[]{:S(2)}, u32[]{:S(2)}) collective-permute-start(bf16[512,2048]{1,0:T(8,128)(2,1)} %convolution_convert_fusion.3), channel_id=1, source_target_pairs={{0,1},{1,0},{2,3},{3,2},{4,5},{5,4},{6,7},{7,6},{8,9},{9,8},{10,11... | collective-permute-start | bytes 6291464 | tf_op jit(solution)/shard_map/ppermute | solution.py:72
  138.3 6.0 %slice-start.3 = ((s8[12582912]{0:T(1024)(128)(4,1)}), s8[4194304]{0:T(1024)(128)(4,1)S(1)}, s32[]{:S(2)}) async-start(s8[12582912]{0:T(1024)(128)(4,1)} %bitcast.87), calls=%async_computation.4 | async-start | bytes 8388608
  138.8 5.5 %slice-start.4 = ((s8[12582912]{0:T(1024)(128)(4,1)}), s8[4194304]{0:T(1024)(128)(4,1)S(1)}, s32[]{:S(2)}) async-start(s8[12582912]{0:T(1024)(128)(4,1)} %bitcast.87), calls=%async_computation.5 | async-start | bytes 8388608
  138.8 5.5 %slice-start.5 = ((s8[12582912]{0:T(1024)(128)(4,1)}), s8[4194304]{0:T(1024)(128)(4,1)S(1)}, s32[]{:S(2)}) async-start(s8[12582912]{0:T(1024)(128)(4,1)} %bitcast.87), calls=%async_computation.6 | async-start | bytes 8388608
  143.5 14.0 %collective-permute-start = (bf16[512,2048]{1,0:T(8,128)(2,1)}, bf16[512,2048]{1,0:T(8,128)(2,1)S(1)}, u32[]{:S(2)}, u32[]{:S(2)}) collective-permute-start(bf16[512,2048]{1,0:T(8,128)(2,1)} %convolution_convert_fusion.1), channel_id=1, source_target_pairs={{0,1},{1,0},{2,3},{3,2},{4,5},{5,4},{6,7},{7,6},{8,9},{9,8},{10,11... | collective-permute-start | bytes 6291464 | tf_op jit(solution)/shard_map/ppermute | solution.py:72
  148.7 47.9 %collective-permute-start.2 = (bf16[512,2048]{1,0:T(8,128)(2,1)S(1)}, bf16[512,2048]{1,0:T(8,128)(2,1)S(1)}, u32[]{:S(2)}, u32[]{:S(2)}) collective-permute-start(bf16[512,2048]{1,0:T(8,128)(2,1)S(1)} %add_convert_fusion.1), channel_id=1, source_target_pairs={{0,2},{1,3},{2,0},{3,1},{4,6},{5,7},{6,4},{7,5},{8,10},{9,11},{10,... | collective-permute-start | bytes 6291464 | tf_op jit(solution)/shard_map/ppermute | solution.py:79
  198.3 9.2 %collective-permute-start.3 = (bf16[128,1024]{1,0:T(8,128)(2,1)S(1)}, bf16[128,1024]{1,0:T(8,128)(2,1)}, u32[]{:S(2)}, u32[]{:S(2)}) collective-permute-start(bf16[128,1024]{1,0:T(8,128)(2,1)S(1)} %get-tuple-element.29), channel_id=1, source_target_pairs={{0,4},{1,5},{2,6},{3,7},{16,20},{17,21},{18,22},{19,23}} | collective-permute-start | bytes 786440 | tf_op jit(solution)/shard_map/ppermute | solution.py:99
  201.6 5.9 %collective-permute-start.6 = (bf16[128,1024]{1,0:T(8,128)(2,1)S(1)}, bf16[128,1024]{1,0:T(8,128)(2,1)}, u32[]{:S(2)}, u32[]{:S(2)}) collective-permute-start(bf16[128,1024]{1,0:T(8,128)(2,1)S(1)} %get-tuple-element.30), channel_id=1, source_target_pairs={{12,8},{13,9},{14,10},{15,11},{28,24},{29,25},{30,26},{31,27}} | collective-permute-start | bytes 786440 | tf_op jit(solution)/shard_map/ppermute | solution.py:100
  203.0 12.3 %collective-permute-start.12 = (bf16[128,1024]{1,0:T(8,128)(2,1)S(1)}, bf16[128,1024]{1,0:T(8,128)(2,1)S(1)}, u32[]{:S(2)}, u32[]{:S(2)}) collective-permute-start(bf16[128,1024]{1,0:T(8,128)(2,1)S(1)} %get-tuple-element.36), channel_id=1, source_target_pairs={{12,8},{13,9},{14,10},{15,11},{28,24},{29,25},{30,26},{31,27}} | collective-permute-start | bytes 786440 | tf_op jit(solution)/shard_map/ppermute | solution.py:100
  203.7 11.6 %collective-permute-start.9 = (bf16[128,1024]{1,0:T(8,128)(2,1)S(1)}, bf16[128,1024]{1,0:T(8,128)(2,1)}, u32[]{:S(2)}, u32[]{:S(2)}) collective-permute-start(bf16[128,1024]{1,0:T(8,128)(2,1)S(1)} %get-tuple-element.35), channel_id=1, source_target_pairs={{0,4},{1,5},{2,6},{3,7},{16,20},{17,21},{18,22},{19,23}} | collective-permute-start | bytes 786440 | tf_op jit(solution)/shard_map/ppermute | solution.py:99
  209.4 13.1 %collective-permute-start.4 = (bf16[128,1024]{1,0:T(8,128)(2,1)}, bf16[128,1024]{1,0:T(8,128)(2,1)S(1)}, u32[]{:S(2)}, u32[]{:S(2)}) collective-permute-start(bf16[128,1024]{1,0:T(8,128)(2,1)} %get-tuple-element.27), channel_id=1, source_target_pairs={{0,4},{1,5},{2,6},{3,7},{4,8},{5,9},{6,10},{7,11},{16,20},{17,21},... | collective-permute-start | bytes 786440 | tf_op jit(solution)/shard_map/ppermute | solution.py:99
  213.9 8.6 %collective-permute-start.7 = (bf16[128,1024]{1,0:T(8,128)(2,1)S(1)}, bf16[128,1024]{1,0:T(8,128)(2,1)}, u32[]{:S(2)}, u32[]{:S(2)}) collective-permute-start(bf16[128,1024]{1,0:T(8,128)(2,1)S(1)} %get-tuple-element.28), channel_id=1, source_target_pairs={{8,4},{9,5},{10,6},{11,7},{12,8},{13,9},{14,10},{15,11},{24,20},{2... | collective-permute-start | bytes 786440 | tf_op jit(solution)/shard_map/ppermute | solution.py:100
  217.2 13.7 %collective-permute-start.10 = (bf16[128,1024]{1,0:T(8,128)(2,1)}, bf16[128,1024]{1,0:T(8,128)(2,1)S(1)}, u32[]{:S(2)}, u32[]{:S(2)}) collective-permute-start(bf16[128,1024]{1,0:T(8,128)(2,1)} %get-tuple-element.33), channel_id=1, source_target_pairs={{0,4},{1,5},{2,6},{3,7},{4,8},{5,9},{6,10},{7,11},{16,20},{17,21},... | collective-permute-start | bytes 786440 | tf_op jit(solution)/shard_map/ppermute | solution.py:99
  221.8 9.0 %collective-permute-start.13 = (bf16[128,1024]{1,0:T(8,128)(2,1)S(1)}, bf16[128,1024]{1,0:T(8,128)(2,1)S(1)}, u32[]{:S(2)}, u32[]{:S(2)}) collective-permute-start(bf16[128,1024]{1,0:T(8,128)(2,1)S(1)} %get-tuple-element.34), channel_id=1, source_target_pairs={{8,4},{9,5},{10,6},{11,7},{12,8},{13,9},{14,10},{15,11},{24,20},{2... | collective-permute-start | bytes 786440 | tf_op jit(solution)/shard_map/ppermute | solution.py:100
  224.4 13.9 %collective-permute-start.5 = (bf16[128,1024]{1,0:T(8,128)(2,1)}, bf16[128,1024]{1,0:T(8,128)(2,1)S(1)}, u32[]{:S(2)}, u32[]{:S(2)}) collective-permute-start(bf16[128,1024]{1,0:T(8,128)(2,1)} %get-tuple-element.25), channel_id=1, source_target_pairs={{0,4},{1,5},{2,6},{3,7},{4,8},{5,9},{6,10},{7,11},{8,12},{9,13},{1... | collective-permute-start | bytes 786440 | tf_op jit(solution)/shard_map/ppermute | solution.py:99
  229.6 10.7 %collective-permute-start.8 = (bf16[128,1024]{1,0:T(8,128)(2,1)S(1)}, bf16[128,1024]{1,0:T(8,128)(2,1)}, u32[]{:S(2)}, u32[]{:S(2)}) collective-permute-start(bf16[128,1024]{1,0:T(8,128)(2,1)S(1)} %get-tuple-element.26), channel_id=1, source_target_pairs={{4,0},{5,1},{6,2},{7,3},{8,4},{9,5},{10,6},{11,7},{12,8},{13,9},{1... | collective-permute-start | bytes 786440 | tf_op jit(solution)/shard_map/ppermute | solution.py:100
  231.8 9.6 %collective-permute-start.11 = (bf16[128,1024]{1,0:T(8,128)(2,1)}, bf16[128,1024]{1,0:T(8,128)(2,1)S(1)}, u32[]{:S(2)}, u32[]{:S(2)}) collective-permute-start(bf16[128,1024]{1,0:T(8,128)(2,1)} %get-tuple-element.31), channel_id=1, source_target_pairs={{0,4},{1,5},{2,6},{3,7},{4,8},{5,9},{6,10},{7,11},{8,12},{9,13},{1... | collective-permute-start | bytes 786440 | tf_op jit(solution)/shard_map/ppermute | solution.py:99
  237.0 8.3 %collective-permute-start.14 = (bf16[128,1024]{1,0:T(8,128)(2,1)S(1)}, bf16[128,1024]{1,0:T(8,128)(2,1)S(1)}, u32[]{:S(2)}, u32[]{:S(2)}) collective-permute-start(bf16[128,1024]{1,0:T(8,128)(2,1)S(1)} %get-tuple-element.32), channel_id=1, source_target_pairs={{4,0},{5,1},{6,2},{7,3},{8,4},{9,5},{10,6},{11,7},{12,8},{13,9},{1... | collective-permute-start | bytes 786440 | tf_op jit(solution)/shard_map/ppermute | solution.py:100
Sparse Core Ops, SparseCore 0:
  10.2 80.8 all-gather.1

commit v3 on v2

v3 whole, which is shorter than its diff:
```python
import functools
import jax
import jax.numpy as jnp
from jax import lax
from jax.sharding import PartitionSpec as P

LANES = 128
CUTS = 2


def apply_experts(rows, shares, gate_up, down_proj):
    exp_dev, half, width = down_proj.shape
    parts = []
    for expert in range(exp_dev):
        projected = jnp.dot(rows, gate_up[expert], preferred_element_type=jnp.float32)
        hidden = jax.nn.silu(projected[:, :half]) * projected[:, half:]
        parts.append((hidden * shares[:, expert : expert + 1]).astype(jnp.bfloat16))
    down = down_proj.reshape(exp_dev * half, width)
    return jnp.dot(
        jnp.concatenate(parts, axis=1), down, preferred_element_type=jnp.float32
    ).astype(jnp.bfloat16)


def gather_small(small, me, n):
    held = small[None]
    bit = 1
    while bit < n:
        other = lax.ppermute(held, "expert", [(i, i ^ bit) for i in range(n)])
        held = jnp.concatenate([held, other], axis=0)
        bit *= 2
    return jnp.take(held, me ^ jnp.arange(n, dtype=jnp.int32), axis=0)


def add(*terms):
    total = terms[0].astype(jnp.float32)
    for term in terms[1:]:
        total = total + term.astype(jnp.float32)
    return total.astype(jnp.bfloat16)


def on_device(y_size, tokens, expert_ids, gate_levels, gate_up, down_proj):
    tok_dev, width = tokens.shape
    top = expert_ids.shape[1]
    n = lax.axis_size("expert")
    z_size = n // (2 * y_size)
    me = lax.axis_index("expert")
    core, y, z = me % 2, (me // 2) % y_size, me // (2 * y_size)
    exp_dev = gate_up.shape[0]
    first = me * exp_dev

    gathered = lax.all_gather(tokens, "expert", axis=0, tiled=True)
    gathered = gathered.reshape(z_size, y_size, 2, tok_dev, width)
    small = jnp.concatenate([expert_ids, gate_levels], axis=1).reshape(-1, LANES)
    small = gather_small(small, me, n).reshape(n * tok_dev, 2 * top)
    ids, levels = small[:, :top], small[:, top:].astype(jnp.float32)
    weights = levels / jnp.sum(levels, axis=1, keepdims=True)
    shares = jnp.stack(
        [
            jnp.sum(jnp.where(ids == first + expert, weights, 0.0), axis=1)
            for expert in range(exp_dev)
        ],
        axis=1,
    ).reshape(z_size, y_size, 2, tok_dev, exp_dev)

    def group(y_to, core_to, after):
        at = (0, y_to, core_to, 0, 0)
        rows = lax.dynamic_slice(gathered, at, (z_size, 1, 1, tok_dev, width))
        share = lax.dynamic_slice(shares, at, (z_size, 1, 1, tok_dev, exp_dev))
        rows = rows.reshape(z_size * tok_dev, width)
        share = share.reshape(z_size * tok_dev, exp_dev)
        if after is not None:
            rows, after = lax.optimization_barrier((rows, after))
        part = apply_experts(rows, share, gate_up, down_proj)
        return part, after

    core_pairs = [(i, i ^ 1) for i in range(n)]
    y_pairs = [(i, i ^ 2) for i in range(n)]
    columns = width // CUTS
    from_y = None
    last = None
    for y_to in [(y + step) % y_size for step in range(1, y_size)] + [y]:
        away, last = group(y_to, 1 - core, last)
        arrived = lax.ppermute(away, "expert", core_pairs)
        kept, _ = group(y_to, core, away)
        last = lax.optimization_barrier(kept)
        cuts = [slice(cut * columns, (cut + 1) * columns) for cut in range(CUTS)]
        if y_to is y:
            totals = []
            for cut in range(CUTS):
                terms = [last[:, cuts[cut]], arrived[:, cuts[cut]]]
                totals.append(add(*terms, *([] if from_y is None else [from_y[cut]])))
        else:
            from_y = [
                lax.ppermute(add(last[:, at], arrived[:, at]), "expert", y_pairs) for at in cuts
            ]

    step_z = 2 * y_size
    outs = []
    for cut in range(CUTS):
        own = totals[cut].reshape(z_size, tok_dev, columns)

        def block(at):
            return lax.dynamic_index_in_dim(own, jnp.clip(at, 0, z_size - 1), 0, keepdims=False)

        up, down = None, None
        for step in range(z_size - 1):
            reach = z_size - 1 - step
            up_block, down_block = block(z + reach), block(z - reach)
            up = up_block if up is None else add(up, up_block)
            down = down_block if down is None else add(down, down_block)
            up_pairs = [(i, i + step_z) for i in range(n) if i // step_z + reach < z_size]
            down_pairs = [(i, i - step_z) for i in range(n) if i // step_z >= reach]
            up = lax.ppermute(up, "expert", up_pairs)
            down = lax.ppermute(down, "expert", down_pairs)
        outs.append(add(block(z), up, down) if z_size > 1 else own[0])
    return jnp.concatenate(outs, axis=1)


def solution(mesh):
    y_size = max(1, 4 // mesh.shape["replica"])
    rows = P(("replica", "expert"), None)
    return jax.shard_map(
        functools.partial(on_device, y_size),
        mesh=mesh,
        in_specs=(rows, rows, rows, P("expert", None, None), P("expert", None, None)),
        out_specs=rows,
        check_vma=False,
    )
```

time: 254 us -> 253 us (level)
  waiting for transfers between devices: 128 us -> 116 us
  starting transfers between devices: 32.7 us -> 43.8 us
    all_gather x1, waiting for transfers between devices: 81 us -> 61.5 us  [on_device(): gathered = lax.all_gather(tokens, 'expert', axis=0, tiled=True)]
    ppermute x1 -> x6, starting transfers between devices: 0.62 us -> 10.6 us  [the longest x4 8.46 us: gather_small(): other = lax.ppermute(held, 'expert', [(i, i ^ bit) for i in range(n)])]
    ppermute x1 -> x6, waiting for transfers between devices: 39.1 us -> 48.8 us  [the longest x2 41.6 us: on_device(): lax.ppermute(add(last[:, at], arrived[:, at]), 'expert', y_pairs)]
    dot_general x4, matrix products: 16.9 us -> 24.1 us  [apply_experts(): jnp.dot(jnp.concatenate(parts, axis=1), down, preferred_element_type=jnp....]
    dot_general x8, matrix products: 36.6 us -> 31.8 us  [apply_experts(): jnp.dot(rows, gate_up[expert], preferred_element_type=jnp.float32)]
    ppermute x6, waiting for transfers between devices: 5.87 us -> 1.51 us  [on_device(): down = lax.ppermute(down, 'expert', down_pairs)]
  transfers between devices with their start and end apart: 16 -> 21, of which waited for: 5 -> 10; matrix products, arithmetic and copies ran while one was open for 11% -> 21% of each run, Pallas kernels for 0% -> 0%
where the time goes in v3:
time: 253 us; the launch traced here: 252 us
  waiting for transfers between devices  116 us (46%)
  matrix products  55.8 us (22%)
  starting transfers between devices  43.8 us (17%)
  other arithmetic  17.3 us (7%)
  between operations  13.9 us (5%)
  local copies, waits for them, and re-layouts  5.54 us (2%)
    all_gather x1, waiting for transfers between devices, on_device(): gathered = lax.all_gather(tokens, 'expert', axis=0, tiled=True)  61.5 us
    ppermute x2, waiting for transfers between devices, on_device(): lax.ppermute(add(last[:, at], arrived[:, at]), 'expert', y_pairs)  41.6 us
    dot_general x8, matrix products, apply_experts(): jnp.dot(rows, gate_up[expert], preferred_element_type=jnp.float32)  31.8 us
    ppermute x6, starting transfers between devices, on_device(): up = lax.ppermute(up, 'expert', up_pairs)  25.3 us
    dot_general x4, matrix products, apply_experts(): jnp.dot(jnp.concatenate(parts, axis=1), down, preferred_element_type=jnp....  24.1 us
    convert_element_type x8, other arithmetic, add(): return total.astype(jnp.bfloat16)  10.2 us
    ppermute x4, starting transfers between devices, gather_small(): other = lax.ppermute(held, 'expert', [(i, i ^ bit) for i in range(n)])  8.46 us
    ppermute x6, starting transfers between devices, on_device(): down = lax.ppermute(down, 'expert', down_pairs)  7.38 us
  transfers between devices with their start and end apart: 21, of which 10 were waited for; matrix products, arithmetic and copies ran while one was open for 21% of the time, Pallas kernels for 0%

profile of v3, /device:TPU:0, one launch (start us, length us, event | category | flops | bytes accessed | tf_op | source)
XLA Modules:
  0.0 252.2 jit_solution(12804385192516376316)
XLA Ops:
  6.5 0.7 all-gather.2.cloned.1.call-update
  7.3 0.7 pad_add_fusion.3
  8.1 0.5 collective-permute-start
  8.8 0.7 collective-permute-done
  9.5 2.9 %collective-permute-start.1 = (s32[2,16,128]{2,1,0:T(8,128)S(1)}, s32[2,16,128]{2,1,0:T(8,128)S(1)}, u32[]{:S(2)}, u32[]{:S(2)}) collective-permute-start(s32[2,16,128]{2,1,0:T(8,128)S(1)} %pad_add_fusion.2), channel_id=1, source_target_pairs={{0,2},{1,3},{2,0},{3,1},{4,6},{5,7},{6,4},{7,5},{8,10},{9,11},{10,... | collective-permute-start | bytes 49160 | tf_op jit(solution)/shard_map/ppermute | solution.py:28
  12.3 1.7 collective-permute-done.1
  14.0 2.1 collective-permute-start.2
  16.1 1.9 collective-permute-done.2
  18.0 3.0 %collective-permute-start.3 = (s32[8,16,128]{2,1,0:T(8,128)S(1)}, s32[8,16,128]{2,1,0:T(8,128)S(1)}, u32[]{:S(2)}, u32[]{:S(2)}) collective-permute-start(s32[8,16,128]{2,1,0:T(8,128)S(1)} %pad_add_fusion), channel_id=1, source_target_pairs={{0,8},{1,9},{2,10},{3,11},{4,12},{5,13},{6,14},{7,15},{8,0},{9,1},... | collective-permute-start | bytes 196616 | tf_op jit(solution)/shard_map/ppermute | solution.py:28
  21.1 2.9 %collective-permute-done.3 = s32[8,16,128]{2,1,0:T(8,128)S(1)} collective-permute-done((s32[8,16,128]{2,1,0:T(8,128)S(1)}, s32[8,16,128]{2,1,0:T(8,128)S(1)}, u32[]{:S(2)}, u32[]{:S(2)}) %collective-permute-start.3) | collective-permute-done | bytes 65568 | tf_op jit(solution)/shard_map/ppermute | solution.py:28
  24.0 0.6 gather_fusion
  24.6 0.3 select_n.103
  25.0 0.6 fusion.53
  25.6 1.2 select_reduce_fusion.1
  26.9 61.5 %all-gather.2.cloned.1.call-done = bf16[2048,2048]{1,0:T(8,128)(2,1)} async-done(((bf16[128,2048]{1,0:T(8,128)(2,1)}), bf16[2048,2048]{1,0:T(8,128)(2,1)}) %all-gather.2.cloned.1.call-update) | async-done | bytes 8388624 | tf_op jit(solution)/shard_map/all_gather | solution.py:51
  88.5 4.3 %constant_dynamic-slice_fusion.3 = (bf16[4,1,1,128,2048]{4,3,2,1,0:T(8,128)(2,1)S(1)}, bf16[4,1,1,128,2048]{4,3,2,1,0:T(8,128)(2,1)S(1)}, bf16[4,1,1,128,2048]{4...) fusion(bf16[4,2,2,128,2048]{4,3,2,1,0:T(8,128)(2,1)} %bitcast.112, s32[]{:T(128)S(6)} %select_n.94, s32[]{:T(128)S(6)} %select_n.96, ...), kind=kLoop, calls=%fused_computation.122 | loop fusion | bytes 16777232 | tf_op jit(solution)/shard_map/dynamic_slice | solution.py:67
  92.8 5.7 %fusion.6 = f32[512,1536]{1,0:T(8,128)S(1)} fusion(bf16[512,2048]{1,0:T(8,128)(2,1)S(1)} %bitcast.127, bf16[2,2048,1536]{2,1,0:T(8,128)(2,1)} %param.8), kind=kOutput, calls=%fused_computation.7 | convolution fusion | flops 3221225472 | bytes 11534336 | tf_op jit(solution)/shard_map/dot_general | solution.py:15
  98.6 5.6 %fusion.14 = f32[512,1536]{1,0:T(8,128)S(1)} fusion(bf16[512,2048]{1,0:T(8,128)(2,1)S(1)} %bitcast.128, bf16[2,2048,1536]{2,1,0:T(8,128)(2,1)} %param.8), kind=kOutput, calls=%fused_computation.15 | convolution fusion | flops 3221225472 | bytes 11534336 | tf_op jit(solution)/shard_map/dot_general | solution.py:15
  104.2 0.9 fusion.37
  105.0 7.0 %convolution_convert_fusion.3 = bf16[512,2048]{1,0:T(8,128)(2,1)S(1)} fusion(bf16[1536,2048]{1,0:T(8,128)(2,1)} %bitcast.149, bf16[512,768]{1,0:T(8,128)(2,1)S(1)} %get-tuple-element.45, bf16[512,768]{1,0:T(8,128)(2,1)S(1)} %get-tuple-element.46), kind=kOutput, calls=%fused_computation.28 | convolution fusion | flops 3225419776 | bytes 9961472 | tf_op jit(solution)/shard_map/dot_general | solution.py:19
  112.0 0.3 collective-permute-start.5
  112.4 3.4 %fusion.4 = f32[512,1536]{1,0:T(8,128)S(1)} fusion(bf16[512,2048]{1,0:T(8,128)(2,1)S(1)} %bitcast.125, bf16[2,2048,1536]{2,1,0:T(8,128)(2,1)S(1)} %bitcast.148), kind=kOutput, calls=%fused_computation.5 | convolution fusion | flops 3221225472 | bytes 11534336 | tf_op jit(solution)/shard_map/dot_general | solution.py:15
  115.8 3.4 %fusion.12 = f32[512,1536]{1,0:T(8,128)S(1)} fusion(bf16[512,2048]{1,0:T(8,128)(2,1)S(1)} %bitcast.126, bf16[2,2048,1536]{2,1,0:T(8,128)(2,1)S(1)} %bitcast.148), kind=kOutput, calls=%fused_computation.13 | convolution fusion | flops 3221225472 | bytes 11534336 | tf_op jit(solution)/shard_map/dot_general | solution.py:15
  119.2 0.5 fusion.33
  119.6 0.5 fusion.35
  120.1 6.8 %convolution_convert_fusion.2 = bf16[512,2048]{1,0:T(8,128)(2,1)S(1)} fusion(bf16[1536,2048]{1,0:T(8,128)(2,1)} %bitcast.150, bf16[512,768]{1,0:T(8,128)(2,1)S(1)} %fusion.33, bf16[512,768]{1,0:T(8,128)(2,1)S(1)} %fusion.35), kind=kOutput, calls=%fused_computation.27 | convolution fusion | flops 3225419776 | bytes 9961472 | tf_op jit(solution)/shard_map/dot_general | solution.py:19
  126.9 3.4 %fusion.2 = f32[512,1536]{1,0:T(8,128)S(1)} fusion(bf16[512,2048]{1,0:T(8,128)(2,1)S(1)} %bitcast.123, bf16[2,2048,1536]{2,1,0:T(8,128)(2,1)S(1)} %bitcast.148), kind=kOutput, calls=%fused_computation.3 | convolution fusion | flops 3221225472 | bytes 11534336 | tf_op jit(solution)/shard_map/dot_general | solution.py:15
  130.3 3.4 %fusion.10 = f32[512,1536]{1,0:T(8,128)S(1)} fusion(bf16[512,2048]{1,0:T(8,128)(2,1)S(1)} %bitcast.124, bf16[2,2048,1536]{2,1,0:T(8,128)(2,1)S(1)} %bitcast.148), kind=kOutput, calls=%fused_computation.11 | convolution fusion | flops 3221225472 | bytes 11534336 | tf_op jit(solution)/shard_map/dot_general | solution.py:15
  133.7 0.5 fusion.29
  134.2 0.5 fusion.31
  134.6 6.6 %convolution_convert_fusion.1 = bf16[512,2048]{1,0:T(8,128)(2,1)S(1)} fusion(bf16[1536,2048]{1,0:T(8,128)(2,1)} %bitcast.151, bf16[512,768]{1,0:T(8,128)(2,1)S(1)} %fusion.29, bf16[512,768]{1,0:T(8,128)(2,1)S(1)} %fusion.31), kind=kOutput, calls=%fused_computation.26 | convolution fusion | flops 3225419776 | bytes 9961472 | tf_op jit(solution)/shard_map/dot_general | solution.py:19
  141.2 0.3 collective-permute-start.4
  141.5 3.4 %fusion = f32[512,1536]{1,0:T(8,128)S(1)} fusion(bf16[512,2048]{1,0:T(8,128)(2,1)S(1)} %bitcast.121, bf16[2,2048,1536]{2,1,0:T(8,128)(2,1)S(1)} %bitcast.148), kind=kOutput, calls=%fused_computation.1 | convolution fusion | flops 3221225472 | bytes 11534336 | tf_op jit(solution)/shard_map/dot_general | solution.py:15
  144.9 3.4 %fusion.8 = f32[512,1536]{1,0:T(8,128)S(1)} fusion(bf16[512,2048]{1,0:T(8,128)(2,1)S(1)} %bitcast.122, bf16[2,2048,1536]{2,1,0:T(8,128)(2,1)S(1)} %bitcast.148), kind=kOutput, calls=%fused_computation.9 | convolution fusion | flops 3221225472 | bytes 11534336 | tf_op jit(solution)/shard_map/dot_general | solution.py:15
  148.4 0.4 fusion.25
  148.8 1.0 add_convert_fusion.3
  149.9 0.6 collective-permute-start.6
  150.5 1.5 collective-permute-start.13
  152.0 0.5 fusion.27
  152.4 3.7 %convolution_convert_fusion = bf16[512,2048]{1,0:T(8,128)(2,1)S(1)} fusion(bf16[1536,2048]{1,0:T(8,128)(2,1)S(1)} %bitcast.154, bf16[512,768]{1,0:T(8,128)(2,1)S(1)} %fusion.25, bf16[512,768]{1,0:T(8,128)(2,1)S(1)} %fusion.27), kind=kOutput, calls=%fused_computation.25 | convolution fusion | flops 3225419776 | bytes 9961472 | tf_op jit(solution)/shard_map/dot_general | solution.py:19
  156.2 19.7 %collective-permute-done.6 = bf16[512,1024]{1,0:T(8,128)(2,1)S(1)} collective-permute-done((bf16[512,1024]{1,0:T(8,128)(2,1)S(1)}, bf16[512,1024]{1,0:T(8,128)(2,1)S(1)}, u32[]{:S(2)}, u32[]{:S(2)}) %collective-permute-start.6) | collective-permute-done | bytes 1048608 | tf_op jit(solution)/shard_map/ppermute | solution.py:94
  175.9 21.8 %collective-permute-done.13 = bf16[512,1024]{1,0:T(8,128)(2,1)S(1)} collective-permute-done((bf16[512,1024]{1,0:T(8,128)(2,1)S(1)}, bf16[512,1024]{1,0:T(8,128)(2,1)S(1)}, u32[]{:S(2)}, u32[]{:S(2)}) %collective-permute-start.13) | collective-permute-done | bytes 1048608 | tf_op jit(solution)/shard_map/ppermute | solution.py:94
  197.7 1.5 add_convert_fusion.2
  199.3 3.5 %collective-permute-start.14 = (bf16[128,1024]{1,0:T(8,128)(2,1)S(1)}, bf16[128,1024]{1,0:T(8,128)(2,1)}, u32[]{:S(2)}, u32[]{:S(2)}) collective-permute-start(bf16[128,1024]{1,0:T(8,128)(2,1)S(1)} %get-tuple-element.35), channel_id=1, source_target_pairs={{0,4},{1,5},{2,6},{3,7},{16,20},{17,21},{18,22},{19,23}} | collective-permute-start | bytes 786440 | tf_op jit(solution)/shard_map/ppermute | solution.py:113
  202.8 1.4 collective-permute-start.17
  204.2 1.3 collective-permute-start.7
  205.5 1.4 collective-permute-start.10
  206.9 1.9 collective-permute-done.14
  208.8 1.9 fusion.57
  210.7 4.5 %collective-permute-start.15 = (bf16[128,1024]{1,0:T(8,128)(2,1)}, bf16[128,1024]{1,0:T(8,128)(2,1)S(1)}, u32[]{:S(2)}, u32[]{:S(2)}) collective-permute-start(bf16[128,1024]{1,0:T(8,128)(2,1)} %get-tuple-element.33), channel_id=1, source_target_pairs={{0,4},{1,5},{2,6},{3,7},{4,8},{5,9},{6,10},{7,11},{16,20},{17,21},... | collective-permute-start | bytes 786440 | tf_op jit(solution)/shard_map/ppermute | solution.py:113
  215.2 1.4 collective-permute-start.18
  216.6 1.8 fusion.63
  218.5 4.4 %collective-permute-start.8 = (bf16[128,1024]{1,0:T(8,128)(2,1)}, bf16[128,1024]{1,0:T(8,128)(2,1)S(1)}, u32[]{:S(2)}, u32[]{:S(2)}) collective-permute-start(bf16[128,1024]{1,0:T(8,128)(2,1)} %get-tuple-element.27), channel_id=1, source_target_pairs={{0,4},{1,5},{2,6},{3,7},{4,8},{5,9},{6,10},{7,11},{16,20},{17,21},... | collective-permute-start | bytes 786440 | tf_op jit(solution)/shard_map/ppermute | solution.py:113
  222.9 0.7 collective-permute-start.11
  223.6 1.9 fusion.56
  225.5 1.3 collective-permute-start.19
  226.8 6.5 %collective-permute-start.16 = (bf16[128,1024]{1,0:T(8,128)(2,1)S(1)}, bf16[128,1024]{1,0:T(8,128)(2,1)}, u32[]{:S(2)}, u32[]{:S(2)}) collective-permute-start(bf16[128,1024]{1,0:T(8,128)(2,1)S(1)} %get-tuple-element.31), channel_id=1, source_target_pairs={{0,4},{1,5},{2,6},{3,7},{4,8},{5,9},{6,10},{7,11},{8,12},{9,13},{1... | collective-permute-start | bytes 786440 | tf_op jit(solution)/shard_map/ppermute | solution.py:113
  233.3 0.9 fusion.62
  234.2 1.3 collective-permute-start.12
  235.5 5.0 %collective-permute-start.9 = (bf16[128,1024]{1,0:T(8,128)(2,1)S(1)}, bf16[128,1024]{1,0:T(8,128)(2,1)S(1)}, u32[]{:S(2)}, u32[]{:S(2)}) collective-permute-start(bf16[128,1024]{1,0:T(8,128)(2,1)S(1)} %get-tuple-element.25), channel_id=1, source_target_pairs={{0,4},{1,5},{2,6},{3,7},{4,8},{5,9},{6,10},{7,11},{8,12},{9,13},{1... | collective-permute-start | bytes 786440 | tf_op jit(solution)/shard_map/ppermute | solution.py:113
  240.5 1.1 fusion.59
  241.6 1.5 collective-permute-done.12
  243.1 1.2 collective-permute-done.9
  244.5 0.8 pad_maximum_fusion
  (50 shorter events, 0.7 us)
Async XLA Ops:
  6.5 82.0 %all-gather.2.cloned.1.call-start = ((), (), s32[]{:S(2)}) async-start(), calls=%async_computation | async-start | bytes 8912896 | tf_op jit(solution)/shard_map/all_gather | solution.py:51
  8.1 1.3 collective-permute-start
  9.5 4.6 %collective-permute-start.1 = (s32[2,16,128]{2,1,0:T(8,128)S(1)}, s32[2,16,128]{2,1,0:T(8,128)S(1)}, u32[]{:S(2)}, u32[]{:S(2)}) collective-permute-start(s32[2,16,128]{2,1,0:T(8,128)S(1)} %pad_add_fusion.2), channel_id=1, source_target_pairs={{0,2},{1,3},{2,0},{3,1},{4,6},{5,7},{6,4},{7,5},{8,10},{9,11},{10,... | collective-permute-start | bytes 49160 | tf_op jit(solution)/shard_map/ppermute | solution.py:28
  14.0 4.0 %collective-permute-start.2 = (s32[4,16,128]{2,1,0:T(8,128)S(1)}, s32[4,16,128]{2,1,0:T(8,128)S(1)}, u32[]{:S(2)}, u32[]{:S(2)}) collective-permute-start(s32[4,16,128]{2,1,0:T(8,128)S(1)} %pad_add_fusion.1), channel_id=1, source_target_pairs={{0,4},{1,5},{2,6},{3,7},{4,0},{5,1},{6,2},{7,3},{8,12},{9,13},{10,... | collective-permute-start | bytes 98312 | tf_op jit(solution)/shard_map/ppermute | solution.py:28
  18.0 5.9 %collective-permute-start.3 = (s32[8,16,128]{2,1,0:T(8,128)S(1)}, s32[8,16,128]{2,1,0:T(8,128)S(1)}, u32[]{:S(2)}, u32[]{:S(2)}) collective-permute-start(s32[8,16,128]{2,1,0:T(8,128)S(1)} %pad_add_fusion), channel_id=1, source_target_pairs={{0,8},{1,9},{2,10},{3,11},{4,12},{5,13},{6,14},{7,15},{8,0},{9,1},... | collective-permute-start | bytes 196616 | tf_op jit(solution)/shard_map/ppermute | solution.py:28
  104.1 8.2 %slice-start = ((s8[12582912]{0:T(1024)(128)(4,1)}), s8[4194304]{0:T(1024)(128)(4,1)S(1)}, s32[]{:S(2)}) async-start(s8[12582912]{0:T(1024)(128)(4,1)} %bitcast.147), calls=%async_computation.1 | async-start | bytes 8388608
  105.0 7.3 %slice-start.1 = ((s8[12582912]{0:T(1024)(128)(4,1)}), s8[4194304]{0:T(1024)(128)(4,1)S(1)}, s32[]{:S(2)}) async-start(s8[12582912]{0:T(1024)(128)(4,1)} %bitcast.147), calls=%async_computation.2 | async-start | bytes 8388608
  105.0 7.3 %slice-start.2 = ((s8[12582912]{0:T(1024)(128)(4,1)}), s8[4194304]{0:T(1024)(128)(4,1)S(1)}, s32[]{:S(2)}) async-start(s8[12582912]{0:T(1024)(128)(4,1)} %bitcast.147), calls=%async_computation.3 | async-start | bytes 8388608
  112.0 36.8 %collective-permute-start.5 = (bf16[512,2048]{1,0:T(8,128)(2,1)S(1)}, bf16[512,2048]{1,0:T(8,128)(2,1)S(1)}, u32[]{:S(2)}, u32[]{:S(2)}) collective-permute-start(bf16[512,2048]{1,0:T(8,128)(2,1)S(1)} %convolution_convert_fusion.3), channel_id=1, source_target_pairs={{0,1},{1,0},{2,3},{3,2},{4,5},{5,4},{6,7},{7,6},{8,9},{9,8},{10,11... | collective-permute-start | bytes 6291464 | tf_op jit(solution)/shard_map/ppermute | solution.py:83
  141.2 15.0 %collective-permute-start.4 = (bf16[512,2048]{1,0:T(8,128)(2,1)S(1)}, bf16[512,2048]{1,0:T(8,128)(2,1)S(1)}, u32[]{:S(2)}, u32[]{:S(2)}) collective-permute-start(bf16[512,2048]{1,0:T(8,128)(2,1)S(1)} %convolution_convert_fusion.1), channel_id=1, source_target_pairs={{0,1},{1,0},{2,3},{3,2},{4,5},{5,4},{6,7},{7,6},{8,9},{9,8},{10,11... | collective-permute-start | bytes 6291464 | tf_op jit(solution)/shard_map/ppermute | solution.py:83
  148.3 4.1 %slice-start.3 = ((s8[6291456]{0:T(1024)(128)(4,1)}), s8[2097152]{0:T(1024)(128)(4,1)S(1)}, s32[]{:S(2)}) async-start(s8[6291456]{0:T(1024)(128)(4,1)} %bitcast.152), calls=%async_computation.4 | async-start | bytes 4194304
  148.8 3.6 %slice-start.4 = ((s8[6291456]{0:T(1024)(128)(4,1)}), s8[4194304]{0:T(1024)(128)(4,1)S(1)}, s32[]{:S(2)}) async-start(s8[6291456]{0:T(1024)(128)(4,1)} %bitcast.152), calls=%async_computation.5 | async-start | bytes 8388608
  149.9 26.1 %collective-permute-start.6 = (bf16[512,1024]{1,0:T(8,128)(2,1)S(1)}, bf16[512,1024]{1,0:T(8,128)(2,1)S(1)}, u32[]{:S(2)}, u32[]{:S(2)}) collective-permute-start(bf16[512,1024]{1,0:T(8,128)(2,1)S(1)} %get-tuple-element.23), channel_id=1, source_target_pairs={{0,2},{1,3},{2,0},{3,1},{4,6},{5,7},{6,4},{7,5},{8,10},{9,11},{10,... | collective-permute-start | bytes 3145736 | tf_op jit(solution)/shard_map/ppermute | solution.py:94
  150.5 47.2 %collective-permute-start.13 = (bf16[512,1024]{1,0:T(8,128)(2,1)S(1)}, bf16[512,1024]{1,0:T(8,128)(2,1)S(1)}, u32[]{:S(2)}, u32[]{:S(2)}) collective-permute-start(bf16[512,1024]{1,0:T(8,128)(2,1)S(1)} %get-tuple-element.24), channel_id=1, source_target_pairs={{0,2},{1,3},{2,0},{3,1},{4,6},{5,7},{6,4},{7,5},{8,10},{9,11},{10,... | collective-permute-start | bytes 3145736 | tf_op jit(solution)/shard_map/ppermute | solution.py:94
  199.3 9.5 %collective-permute-start.14 = (bf16[128,1024]{1,0:T(8,128)(2,1)S(1)}, bf16[128,1024]{1,0:T(8,128)(2,1)}, u32[]{:S(2)}, u32[]{:S(2)}) collective-permute-start(bf16[128,1024]{1,0:T(8,128)(2,1)S(1)} %get-tuple-element.35), channel_id=1, source_target_pairs={{0,4},{1,5},{2,6},{3,7},{16,20},{17,21},{18,22},{19,23}} | collective-permute-start | bytes 786440 | tf_op jit(solution)/shard_map/ppermute | solution.py:113
  202.8 6.1 %collective-permute-start.17 = (bf16[128,1024]{1,0:T(8,128)(2,1)S(1)}, bf16[128,1024]{1,0:T(8,128)(2,1)}, u32[]{:S(2)}, u32[]{:S(2)}) collective-permute-start(bf16[128,1024]{1,0:T(8,128)(2,1)S(1)} %get-tuple-element.36), channel_id=1, source_target_pairs={{12,8},{13,9},{14,10},{15,11},{28,24},{29,25},{30,26},{31,27}} | collective-permute-start | bytes 786440 | tf_op jit(solution)/shard_map/ppermute | solution.py:114
  204.2 12.5 %collective-permute-start.7 = (bf16[128,1024]{1,0:T(8,128)(2,1)S(1)}, bf16[128,1024]{1,0:T(8,128)(2,1)S(1)}, u32[]{:S(2)}, u32[]{:S(2)}) collective-permute-start(bf16[128,1024]{1,0:T(8,128)(2,1)S(1)} %get-tuple-element.29), channel_id=1, source_target_pairs={{0,4},{1,5},{2,6},{3,7},{16,20},{17,21},{18,22},{19,23}} | collective-permute-start | bytes 786440 | tf_op jit(solution)/shard_map/ppermute | solution.py:113
  205.5 11.2 %collective-permute-start.10 = (bf16[128,1024]{1,0:T(8,128)(2,1)S(1)}, bf16[128,1024]{1,0:T(8,128)(2,1)}, u32[]{:S(2)}, u32[]{:S(2)}) collective-permute-start(bf16[128,1024]{1,0:T(8,128)(2,1)S(1)} %get-tuple-element.30), channel_id=1, source_target_pairs={{12,8},{13,9},{14,10},{15,11},{28,24},{29,25},{30,26},{31,27}} | collective-permute-start | bytes 786440 | tf_op jit(solution)/shard_map/ppermute | solution.py:114
  210.7 12.9 %collective-permute-start.15 = (bf16[128,1024]{1,0:T(8,128)(2,1)}, bf16[128,1024]{1,0:T(8,128)(2,1)S(1)}, u32[]{:S(2)}, u32[]{:S(2)}) collective-permute-start(bf16[128,1024]{1,0:T(8,128)(2,1)} %get-tuple-element.33), channel_id=1, source_target_pairs={{0,4},{1,5},{2,6},{3,7},{4,8},{5,9},{6,10},{7,11},{16,20},{17,21},... | collective-permute-start | bytes 786440 | tf_op jit(solution)/shard_map/ppermute | solution.py:113
  215.2 8.4 %collective-permute-start.18 = (bf16[128,1024]{1,0:T(8,128)(2,1)S(1)}, bf16[128,1024]{1,0:T(8,128)(2,1)}, u32[]{:S(2)}, u32[]{:S(2)}) collective-permute-start(bf16[128,1024]{1,0:T(8,128)(2,1)S(1)} %get-tuple-element.34), channel_id=1, source_target_pairs={{8,4},{9,5},{10,6},{11,7},{12,8},{13,9},{14,10},{15,11},{24,20},{2... | collective-permute-start | bytes 786440 | tf_op jit(solution)/shard_map/ppermute | solution.py:114
  218.5 14.8 %collective-permute-start.8 = (bf16[128,1024]{1,0:T(8,128)(2,1)}, bf16[128,1024]{1,0:T(8,128)(2,1)S(1)}, u32[]{:S(2)}, u32[]{:S(2)}) collective-permute-start(bf16[128,1024]{1,0:T(8,128)(2,1)} %get-tuple-element.27), channel_id=1, source_target_pairs={{0,4},{1,5},{2,6},{3,7},{4,8},{5,9},{6,10},{7,11},{16,20},{17,21},... | collective-permute-start | bytes 786440 | tf_op jit(solution)/shard_map/ppermute | solution.py:113
  222.9 10.4 %collective-permute-start.11 = (bf16[128,1024]{1,0:T(8,128)(2,1)S(1)}, bf16[128,1024]{1,0:T(8,128)(2,1)S(1)}, u32[]{:S(2)}, u32[]{:S(2)}) collective-permute-start(bf16[128,1024]{1,0:T(8,128)(2,1)S(1)} %get-tuple-element.28), channel_id=1, source_target_pairs={{8,4},{9,5},{10,6},{11,7},{12,8},{13,9},{14,10},{15,11},{24,20},{2... | collective-permute-start | bytes 786440 | tf_op jit(solution)/shard_map/ppermute | solution.py:114
  225.5 15.0 %collective-permute-start.19 = (bf16[128,1024]{1,0:T(8,128)(2,1)}, bf16[128,1024]{1,0:T(8,128)(2,1)S(1)}, u32[]{:S(2)}, u32[]{:S(2)}) collective-permute-start(bf16[128,1024]{1,0:T(8,128)(2,1)} %get-tuple-element.32), channel_id=1, source_target_pairs={{4,0},{5,1},{6,2},{7,3},{8,4},{9,5},{10,6},{11,7},{12,8},{13,9},{1... | collective-permute-start | bytes 786440 | tf_op jit(solution)/shard_map/ppermute | solution.py:114
  226.8 13.7 %collective-permute-start.16 = (bf16[128,1024]{1,0:T(8,128)(2,1)S(1)}, bf16[128,1024]{1,0:T(8,128)(2,1)}, u32[]{:S(2)}, u32[]{:S(2)}) collective-permute-start(bf16[128,1024]{1,0:T(8,128)(2,1)S(1)} %get-tuple-element.31), channel_id=1, source_target_pairs={{0,4},{1,5},{2,6},{3,7},{4,8},{5,9},{6,10},{7,11},{8,12},{9,13},{1... | collective-permute-start | bytes 786440 | tf_op jit(solution)/shard_map/ppermute | solution.py:113
  234.2 8.9 %collective-permute-start.12 = (bf16[128,1024]{1,0:T(8,128)(2,1)}, bf16[128,1024]{1,0:T(8,128)(2,1)S(1)}, u32[]{:S(2)}, u32[]{:S(2)}) collective-permute-start(bf16[128,1024]{1,0:T(8,128)(2,1)} %get-tuple-element.26), channel_id=1, source_target_pairs={{4,0},{5,1},{6,2},{7,3},{8,4},{9,5},{10,6},{11,7},{12,8},{13,9},{1... | collective-permute-start | bytes 786440 | tf_op jit(solution)/shard_map/ppermute | solution.py:114
  235.5 8.9 %collective-permute-start.9 = (bf16[128,1024]{1,0:T(8,128)(2,1)S(1)}, bf16[128,1024]{1,0:T(8,128)(2,1)S(1)}, u32[]{:S(2)}, u32[]{:S(2)}) collective-permute-start(bf16[128,1024]{1,0:T(8,128)(2,1)S(1)} %get-tuple-element.25), channel_id=1, source_target_pairs={{0,4},{1,5},{2,6},{3,7},{4,8},{5,9},{6,10},{7,11},{8,12},{9,13},{1... | collective-permute-start | bytes 786440 | tf_op jit(solution)/shard_map/ppermute | solution.py:113
Sparse Core Ops, SparseCore 0:
  9.5 78.9 all-gather.1

commit v4 on v3

--- a/solution.py
+++ b/solution.py
@@ -48,8 +48,6 @@
     exp_dev = gate_up.shape[0]
     first = me * exp_dev
 
-    gathered = lax.all_gather(tokens, "expert", axis=0, tiled=True)
-    gathered = gathered.reshape(z_size, y_size, 2, tok_dev, width)
     small = jnp.concatenate([expert_ids, gate_levels], axis=1).reshape(-1, LANES)
     small = gather_small(small, me, n).reshape(n * tok_dev, 2 * top)
     ids, levels = small[:, :top], small[:, top:].astype(jnp.float32)
@@ -62,39 +60,68 @@
         axis=1,
     ).reshape(z_size, y_size, 2, tok_dev, exp_dev)
 
-    def group(y_to, core_to, after):
-        at = (0, y_to, core_to, 0, 0)
-        rows = lax.dynamic_slice(gathered, at, (z_size, 1, 1, tok_dev, width))
+    core_pairs = [(i, i ^ 1) for i in range(n)]
+    y_pairs = [(i, i ^ 2) for i in range(n)]
+    step_z = 2 * y_size
+    up, down = tokens, tokens
+    line = [tokens]
+    across = [lax.ppermute(tokens, "expert", y_pairs)] if y_size > 1 else []
+    for step in range(1, z_size):
+        up = lax.ppermute(up, "expert", [(i, i + step_z) for i in range(n - step_z)])
+        down = lax.ppermute(down, "expert", [(i + step_z, i) for i in range(n - step_z)])
+        line = [up] + line + [down]
+        if y_size > 1:
+            have_up = [(i, i ^ 2) for i in range(n) if i // step_z >= step]
+            have_down = [(i, i ^ 2) for i in range(n) if i // step_z + step < z_size]
+            across = (
+                [lax.ppermute(up, "expert", have_up)]
+                + across
+                + [lax.ppermute(down, "expert", have_down)]
+            )
+
+    def assemble(blocks):
+        start = (z_size - 1 - z) * tok_dev
+        return lax.dynamic_slice_in_dim(
+            jnp.concatenate(blocks, axis=0), start, z_size * tok_dev, axis=0
+        )
+
+    own_line = assemble(line)
+    lines = {0: (own_line, lax.ppermute(own_line, "expert", core_pairs))}
+
+    def group(y_step, core_step, after):
+        at = (0, (y + y_step) % y_size, (core + core_step) % 2, 0, 0)
+        rows = lines[y_step][core_step]
         share = lax.dynamic_slice(shares, at, (z_size, 1, 1, tok_dev, exp_dev))
-        rows = rows.reshape(z_size * tok_dev, width)
         share = share.reshape(z_size * tok_dev, exp_dev)
         if after is not None:
             rows, after = lax.optimization_barrier((rows, after))
         part = apply_experts(rows, share, gate_up, down_proj)
         return part, after
 
-    core_pairs = [(i, i ^ 1) for i in range(n)]
-    y_pairs = [(i, i ^ 2) for i in range(n)]
     columns = width // CUTS
+    cuts = [slice(cut * columns, (cut + 1) * columns) for cut in range(CUTS)]
+    kept_own, _ = group(0, 0, None)
+    last = kept_own
     from_y = None
-    last = None
-    for y_to in [(y + step) % y_size for step in range(1, y_size)] + [y]:
-        away, last = group(y_to, 1 - core, last)
+    if y_size > 1:
+        across, kept_own = lax.optimization_barrier((across, kept_own))
+        other = assemble(across)
+        lines[1] = (other, lax.ppermute(other, "expert", core_pairs))
+        away, kept_own = group(1, 1, kept_own)
         arrived = lax.ppermute(away, "expert", core_pairs)
-        kept, _ = group(y_to, core, away)
-        last = lax.optimization_barrier(kept)
-        cuts = [slice(cut * columns, (cut + 1) * columns) for cut in range(CUTS)]
-        if y_to is y:
-            totals = []
-            for cut in range(CUTS):
-                terms = [last[:, cuts[cut]], arrived[:, cuts[cut]]]
-                totals.append(add(*terms, *([] if from_y is None else [from_y[cut]])))
-        else:
-            from_y = [
-                lax.ppermute(add(last[:, at], arrived[:, at]), "expert", y_pairs) for at in cuts
-            ]
+        kept, _ = group(1, 0, away)
+        kept = lax.optimization_barrier(kept)
+        last = [add(kept[:, at], arrived[:, at]) for at in cuts]
+        from_y = [lax.ppermute(part, "expert", y_pairs) for part in last]
+        away, from_y[0] = group(0, 1, from_y[0])
+    else:
+        away, kept_own = group(0, 1, kept_own)
+    arrived = lax.ppermute(away, "expert", core_pairs)
+    totals = []
+    for cut, at in enumerate(cuts):
+        terms = [kept_own[:, at], arrived[:, at]]
+        totals.append(add(*terms, *([] if from_y is None else [from_y[cut]])))
 
-    step_z = 2 * y_size
     outs = []
     for cut in range(CUTS):
         own = totals[cut].reshape(z_size, tok_dev, columns)

time: 253 us -> 235 us (0.929)
  starting transfers between devices: 43.8 us -> 74.1 us
  waiting for transfers between devices: 116 us -> 88.5 us
  between operations: 13.9 us -> 0.9 us
  matrix products: 55.8 us -> 46.9 us
    all_gather x1 -> x0, waiting for transfers between devices: 61.5 us -> none  [on_device(): gathered = lax.all_gather(tokens, 'expert', axis=0, tiled=True)]
    ppermute x2 -> x17, starting transfers between devices: 2.09 us -> 35.2 us  [the longest x3 13.4 us: on_device(): lax.ppermute(up, 'expert', [(i, i + step_z) for i in range(n - step_z)])]
    ppermute x2 -> x17, waiting for transfers between devices: 41.6 us -> 61.6 us  [the longest x2 47.9 us: on_device(): from_y = [lax.ppermute(part, 'expert', y_pairs) for part in last]]
    ppermute x4, waiting for transfers between devices: 7.22 us -> 19.2 us  [gather_small(): other = lax.ppermute(held, 'expert', [(i, i ^ bit) for i in range(n)])]
    dot_general x4, matrix products: 24.1 us -> 17.2 us  [apply_experts(): jnp.dot(jnp.concatenate(parts, axis=1), down, preferred_element_type=jnp....]
    dynamic_slice x1 -> x2, local copies, waits for them, and re-layouts: 4.32 us -> 0.29 us  [assemble(): lax.dynamic_slice_in_dim(jnp.concatenate(blocks, axis=0), start, z_size *...]
    ppermute x6, waiting for transfers between devices: 1.51 us -> 4.78 us  [on_device(): down = lax.ppermute(down, 'expert', down_pairs)]
  transfers between devices with their start and end apart: 21 -> 35, of which waited for: 10 -> 13; matrix products, arithmetic and copies ran while one was open for 21% -> 22% of each run, Pallas kernels for 0% -> 0%
where the time goes in v4:
time: 235 us; the launch traced here: 234 us
  waiting for transfers between devices  88.5 us (38%)
  starting transfers between devices  74.1 us (32%)
  matrix products  46.9 us (20%)
  other arithmetic  19.7 us (8%)
  local copies, waits for them, and re-layouts  3.67 us (2%)
    ppermute x2, waiting for transfers between devices, on_device(): from_y = [lax.ppermute(part, 'expert', y_pairs) for part in last]  47.9 us
    dot_general x8, matrix products, apply_experts(): jnp.dot(rows, gate_up[expert], preferred_element_type=jnp.float32)  29.7 us
    ppermute x6, starting transfers between devices, on_device(): up = lax.ppermute(up, 'expert', up_pairs)  25.4 us
    ppermute x4, waiting for transfers between devices, gather_small(): other = lax.ppermute(held, 'expert', [(i, i ^ bit) for i in range(n)])  19.2 us
    dot_general x4, matrix products, apply_experts(): jnp.dot(jnp.concatenate(parts, axis=1), down, preferred_element_type=jnp....  17.2 us
    ppermute x3, starting transfers between devices, on_device(): lax.ppermute(up, 'expert', [(i, i + step_z) for i in range(n - step_z)])  13.4 us
    convert_element_type x8, other arithmetic, add(): return total.astype(jnp.bfloat16)  12.6 us
    ppermute x3, starting transfers between devices, on_device(): lax.ppermute(down, 'expert', have_down)  10.3 us
  transfers between devices with their start and end apart: 35, of which 13 were waited for; matrix products, arithmetic and copies ran while one was open for 22% of the time, Pallas kernels for 0%

profile of v4, /device:TPU:0, one launch (start us, length us, event | category | flops | bytes accessed | tf_op | source)
XLA Modules:
  0.0 233.8 jit_solution(3470186054600232304)
XLA Ops:
  0.0 5.0 %collective-permute-start = (bf16[128,2048]{1,0:T(8,128)(2,1)}, bf16[128,2048]{1,0:T(8,128)(2,1)S(1)}, u32[]{:S(2)}, u32[]{:S(2)}) collective-permute-start(bf16[128,2048]{1,0:T(8,128)(2,1)} %param.5), channel_id=1, source_target_pairs={{0,4},{1,5},{2,6},{3,7},{4,8},{5,9},{6,10},{7,11},{8,12},{9,13},{1... | collective-permute-start | bytes 1572872 | tf_op jit(solution)/shard_map/ppermute | solution.py:70
  5.0 1.3 collective-permute-start.7
  6.3 1.6 collective-permute-start.6
  7.8 0.7 pad_add_fusion.3
  9.0 1.0 collective-permute-done.13
  10.5 9.8 %collective-permute-done.14 = s32[2,16,128]{2,1,0:T(8,128)S(1)} collective-permute-done((s32[2,16,128]{2,1,0:T(8,128)S(1)}, s32[2,16,128]{2,1,0:T(8,128)S(1)}, u32[]{:S(2)}, u32[]{:S(2)}) %collective-permute-start.14) | collective-permute-done | bytes 16416 | tf_op jit(solution)/shard_map/ppermute | solution.py:28
  20.3 2.4 %collective-permute-start.15 = (s32[4,16,128]{2,1,0:T(8,128)S(1)}, s32[4,16,128]{2,1,0:T(8,128)S(1)}, u32[]{:S(2)}, u32[]{:S(2)}) collective-permute-start(s32[4,16,128]{2,1,0:T(8,128)S(1)} %pad_add_fusion.1), channel_id=1, source_target_pairs={{0,4},{1,5},{2,6},{3,7},{4,0},{5,1},{6,2},{7,3},{8,12},{9,13},{10,... | collective-permute-start | bytes 98312 | tf_op jit(solution)/shard_map/ppermute | solution.py:28
  22.6 1.9 collective-permute-start.1
  24.6 3.0 %collective-permute-start.16 = (s32[8,16,128]{2,1,0:T(8,128)S(1)}, s32[8,16,128]{2,1,0:T(8,128)S(1)}, u32[]{:S(2)}, u32[]{:S(2)}) collective-permute-start(s32[8,16,128]{2,1,0:T(8,128)S(1)} %pad_add_fusion), channel_id=1, source_target_pairs={{0,8},{1,9},{2,10},{3,11},{4,12},{5,13},{6,14},{7,15},{8,0},{9,1},... | collective-permute-start | bytes 196616 | tf_op jit(solution)/shard_map/ppermute | solution.py:28
  27.7 8.3 %collective-permute-done.16 = s32[8,16,128]{2,1,0:T(8,128)S(1)} collective-permute-done((s32[8,16,128]{2,1,0:T(8,128)S(1)}, s32[8,16,128]{2,1,0:T(8,128)S(1)}, u32[]{:S(2)}, u32[]{:S(2)}) %collective-permute-start.16) | collective-permute-done | bytes 65568 | tf_op jit(solution)/shard_map/ppermute | solution.py:28
  37.0 1.3 collective-permute-start.9
  38.3 6.5 %collective-permute-start.2 = (bf16[128,2048]{1,0:T(8,128)(2,1)S(1)}, bf16[128,2048]{1,0:T(8,128)(2,1)S(1)}, u32[]{:S(2)}, u32[]{:S(2)}) collective-permute-start(bf16[128,2048]{1,0:T(8,128)(2,1)S(1)} %collective-permute-done.1), channel_id=1, source_target_pairs={{0,4},{1,5},{2,6},{3,7},{4,8},{5,9},{6,10},{7,11},{8,12},{9,13},{1... | collective-permute-start | bytes 1572872 | tf_op jit(solution)/shard_map/ppermute | solution.py:70
  45.4 1.2 select_reduce_fusion.1
  46.7 0.8 collective-permute-start.5
  47.5 3.4 %collective-permute-start.8 = (bf16[128,2048]{1,0:T(8,128)(2,1)S(1)}, bf16[128,2048]{1,0:T(8,128)(2,1)S(1)}, u32[]{:S(2)}, u32[]{:S(2)}) collective-permute-start(bf16[128,2048]{1,0:T(8,128)(2,1)S(1)} %collective-permute-done.7), channel_id=1, source_target_pairs={{0,2},{1,3},{2,0},{3,1},{4,6},{5,7},{6,4},{7,5},{8,10},{9,11},{10,... | collective-permute-start | bytes 1572872 | tf_op jit(solution)/shard_map/ppermute | solution.py:79
  51.3 1.3 collective-permute-start.11
  52.6 3.4 %collective-permute-start.10 = (bf16[128,2048]{1,0:T(8,128)(2,1)S(1)}, bf16[128,2048]{1,0:T(8,128)(2,1)S(1)}, u32[]{:S(2)}, u32[]{:S(2)}) collective-permute-start(bf16[128,2048]{1,0:T(8,128)(2,1)S(1)} %collective-permute-done.9), channel_id=1, source_target_pairs={{0,2},{1,3},{2,0},{3,1},{4,6},{5,7},{6,4},{7,5},{16,18},{17,19},{1... | collective-permute-start | bytes 1572872 | tf_op jit(solution)/shard_map/ppermute | solution.py:79
  56.3 7.7 %collective-permute-done.11 = bf16[128,2048]{1,0:T(8,128)(2,1)S(1)} collective-permute-done((bf16[128,2048]{1,0:T(8,128)(2,1)S(1)}, bf16[128,2048]{1,0:T(8,128)(2,1)S(1)}, u32[]{:S(2)}, u32[]{:S(2)}) %collective-permute-start.11) | collective-permute-done | bytes 524320 | tf_op jit(solution)/shard_map/ppermute | solution.py:71
  64.0 0.7 collective-permute-start.4
  65.0 5.7 %fusion.14 = f32[512,1536]{1,0:T(8,128)S(1)} fusion(bf16[512,2048]{1,0:T(8,128)(2,1)S(1)} %constant_dynamic-slice_fusion.1, bf16[2,2048,1536]{2,1,0:T(8,128)(2,1)} %param.8), kind=kOutput, calls=%fused_computation.15 | convolution fusion | flops 3221225472 | bytes 11534336 | tf_op jit(solution)/shard_map/dot_general | solution.py:15
  71.3 3.4 %fusion.6 = f32[512,1536]{1,0:T(8,128)S(1)} fusion(bf16[512,2048]{1,0:T(8,128)(2,1)S(1)} %constant_dynamic-slice_fusion.1, bf16[2,2048,1536]{2,1,0:T(8,128)(2,1)S(1)} %bitcast.134), kind=kOutput, calls=%fused_computation.7 | convolution fusion | flops 3221225472 | bytes 11534336 | tf_op jit(solution)/shard_map/dot_general | solution.py:15
  74.8 0.9 fusion.37
  75.6 3.4 %collective-permute-start.12 = (bf16[128,2048]{1,0:T(8,128)(2,1)S(1)}, bf16[128,2048]{1,0:T(8,128)(2,1)S(1)}, u32[]{:S(2)}, u32[]{:S(2)}) collective-permute-start(bf16[128,2048]{1,0:T(8,128)(2,1)S(1)} %collective-permute-done.11), channel_id=1, source_target_pairs={{0,2},{1,3},{2,0},{3,1},{16,18},{17,19},{18,16},{19,17}} | collective-permute-start | bytes 1572872 | tf_op jit(solution)/shard_map/ppermute | solution.py:79
  79.1 0.9 collective-permute-start.3
  80.0 4.7 %convolution_convert_fusion.3 = bf16[512,2048]{1,0:T(8,128)(2,1)} fusion(bf16[1536,2048]{1,0:T(8,128)(2,1)S(1)} %bitcast.137, bf16[512,768]{1,0:T(8,128)(2,1)S(1)} %get-tuple-element.61, bf16[512,768]{1,0:T(8,128)(2,1)S(1)} %get-tuple-element.62), kind=kOutput, calls=%fused_computation.28 | convolution fusion | flops 3225419776 | bytes 9961472 | tf_op jit(solution)/shard_map/dot_general | solution.py:19
  84.7 2.0 collective-permute-done.12
  87.8 3.6 %collective-permute-done.17 = bf16[512,2048]{1,0:T(8,128)(2,1)S(1)} collective-permute-done((bf16[512,2048]{1,0:T(8,128)(2,1)S(1)}, bf16[512,2048]{1,0:T(8,128)(2,1)S(1)}, u32[]{:S(2)}, u32[]{:S(2)}) %collective-permute-start.17) | collective-permute-done | bytes 2097184 | tf_op jit(solution)/shard_map/ppermute | solution.py:109
  91.4 3.4 %fusion.12 = f32[512,1536]{1,0:T(8,128)S(1)} fusion(bf16[512,2048]{1,0:T(8,128)(2,1)S(1)} %collective-permute-done.17, bf16[2,2048,1536]{2,1,0:T(8,128)(2,1)S(1)} %bitcast.134), kind=kOutput, calls=%fused_computation.13 | convolution fusion | flops 3221225472 | bytes 11534336 | tf_op jit(solution)/shard_map/dot_general | solution.py:15
  94.8 3.4 %fusion.4 = f32[512,1536]{1,0:T(8,128)S(1)} fusion(bf16[512,2048]{1,0:T(8,128)(2,1)S(1)} %collective-permute-done.17, bf16[2,2048,1536]{2,1,0:T(8,128)(2,1)S(1)} %bitcast.134), kind=kOutput, calls=%fused_computation.5 | convolution fusion | flops 3221225472 | bytes 11534336 | tf_op jit(solution)/shard_map/dot_general | solution.py:15
  99.2 3.9 %convolution_convert_fusion.2 = bf16[512,2048]{1,0:T(8,128)(2,1)S(1)} fusion(bf16[1536,2048]{1,0:T(8,128)(2,1)S(1)} %bitcast.138, bf16[512,768]{1,0:T(8,128)(2,1)S(1)} %fusion.33, bf16[512,768]{1,0:T(8,128)(2,1)S(1)} %fusion.35), kind=kOutput, calls=%fused_computation.27 | convolution fusion | flops 3225419776 | bytes 9961472 | tf_op jit(solution)/shard_map/dot_general | solution.py:19
  103.3 3.4 %fusion.10 = f32[512,1536]{1,0:T(8,128)S(1)} fusion(bf16[512,2048]{1,0:T(8,128)(2,1)S(1)} %constant_dynamic-slice_fusion, bf16[2,2048,1536]{2,1,0:T(8,128)(2,1)S(1)} %bitcast.134), kind=kOutput, calls=%fused_computation.11 | convolution fusion | flops 3221225472 | bytes 11534336 | tf_op jit(solution)/shard_map/dot_general | solution.py:15
  107.2 3.4 %fusion.2 = f32[512,1536]{1,0:T(8,128)S(1)} fusion(bf16[512,2048]{1,0:T(8,128)(2,1)S(1)} %constant_dynamic-slice_fusion, bf16[2,2048,1536]{2,1,0:T(8,128)(2,1)S(1)} %bitcast.134), kind=kOutput, calls=%fused_computation.3 | convolution fusion | flops 3221225472 | bytes 11534336 | tf_op jit(solution)/shard_map/dot_general | solution.py:15
  111.1 3.7 %convolution_convert_fusion.1 = bf16[512,2048]{1,0:T(8,128)(2,1)S(1)} fusion(bf16[1536,2048]{1,0:T(8,128)(2,1)S(1)} %bitcast.139, bf16[512,768]{1,0:T(8,128)(2,1)S(1)} %fusion.29, bf16[512,768]{1,0:T(8,128)(2,1)S(1)} %fusion.31), kind=kOutput, calls=%fused_computation.26 | convolution fusion | flops 3225419776 | bytes 9961472 | tf_op jit(solution)/shard_map/dot_general | solution.py:19
  114.7 1.0 add_convert_fusion.3
  115.7 1.6 collective-permute-start.20
  117.3 23.9 %collective-permute-done.20 = bf16[512,1024]{1,0:T(8,128)(2,1)S(1)} collective-permute-done((bf16[512,1024]{1,0:T(8,128)(2,1)S(1)}, bf16[512,1024]{1,0:T(8,128)(2,1)S(1)}, u32[]{:S(2)}, u32[]{:S(2)}) %collective-permute-start.20) | collective-permute-done | bytes 1048608 | tf_op jit(solution)/shard_map/ppermute | solution.py:115
  141.2 3.4 %fusion.8 = f32[512,1536]{1,0:T(8,128)S(1)} fusion(bf16[512,2048]{1,0:T(8,128)(2,1)S(1)} %collective-permute-done.18, bf16[2,2048,1536]{2,1,0:T(8,128)(2,1)S(1)} %bitcast.134), kind=kOutput, calls=%fused_computation.9 | convolution fusion | flops 3221225472 | bytes 11534336 | tf_op jit(solution)/shard_map/dot_general | solution.py:15
  144.7 3.4 %fusion = f32[512,1536]{1,0:T(8,128)S(1)} fusion(bf16[512,2048]{1,0:T(8,128)(2,1)S(1)} %collective-permute-done.18, bf16[2,2048,1536]{2,1,0:T(8,128)(2,1)S(1)} %bitcast.134), kind=kOutput, calls=%fused_computation.1 | convolution fusion | flops 3221225472 | bytes 11534336 | tf_op jit(solution)/shard_map/dot_general | solution.py:15
  149.0 5.0 %convolution_convert_fusion = bf16[512,2048]{1,0:T(8,128)(2,1)} fusion(bf16[1536,2048]{1,0:T(8,128)(2,1)S(1)} %bitcast.140, bf16[512,768]{1,0:T(8,128)(2,1)S(1)} %fusion.25, bf16[512,768]{1,0:T(8,128)(2,1)S(1)} %fusion.27), kind=kOutput, calls=%fused_computation.25 | convolution fusion | flops 3225419776 | bytes 9961472 | tf_op jit(solution)/shard_map/dot_general | solution.py:19
  154.0 1.5 collective-permute-start.28
  155.5 24.1 %collective-permute-done.28 = bf16[512,1024]{1,0:T(8,128)(2,1)S(1)} collective-permute-done((bf16[512,1024]{1,0:T(8,128)(2,1)S(1)}, bf16[512,1024]{1,0:T(8,128)(2,1)S(1)}, u32[]{:S(2)}, u32[]{:S(2)}) %collective-permute-start.28) | collective-permute-done | bytes 1048608 | tf_op jit(solution)/shard_map/ppermute | solution.py:115
  179.6 1.0 copy-done
  180.5 4.0 %add_convert_fusion.2 = (bf16[512,1024]{1,0:T(8,128)(2,1)S(1)}, bf16[512,1024]{1,0:T(8,128)(2,1)S(1)}) fusion(bf16[512,1024]{1,0:T(8,128)(2,1)S(1)} %collective-permute-done.20, bf16[512,2048]{1,0:T(8,128)(2,1)} %collective-permute-done.21, bf16[512,2048]{1,0:T(8,128)(2,1)} %convolution_convert_fusion.3, bf16[512,1024]{1,0:T(8,128)(2,1)} %copy-done), kind=kLoop, calls=%fused_computation.31 | loop fusion | flops 6291456 | bytes 8388608 | tf_op jit(solution)/shard_map/convert_element_type | solution.py:38
  184.5 2.0 collective-permute-start.22
  186.5 1.4 collective-permute-start.25
  187.9 1.3 collective-permute-start.29
  189.2 1.4 collective-permute-start.32
  190.6 1.9 collective-permute-done.22
  192.5 1.9 fusion.63
  194.4 4.5 %collective-permute-start.23 = (bf16[128,1024]{1,0:T(8,128)(2,1)}, bf16[128,1024]{1,0:T(8,128)(2,1)S(1)}, u32[]{:S(2)}, u32[]{:S(2)}) collective-permute-start(bf16[128,1024]{1,0:T(8,128)(2,1)} %get-tuple-element.43), channel_id=1, source_target_pairs={{0,4},{1,5},{2,6},{3,7},{4,8},{5,9},{6,10},{7,11},{16,20},{17,21},... | collective-permute-start | bytes 786440 | tf_op jit(solution)/shard_map/ppermute | solution.py:140
  198.9 1.4 collective-permute-start.26
  200.3 1.8 fusion.57
  202.2 7.3 %collective-permute-start.30 = (bf16[128,1024]{1,0:T(8,128)(2,1)}, bf16[128,1024]{1,0:T(8,128)(2,1)S(1)}, u32[]{:S(2)}, u32[]{:S(2)}) collective-permute-start(bf16[128,1024]{1,0:T(8,128)(2,1)} %get-tuple-element.49), channel_id=1, source_target_pairs={{0,4},{1,5},{2,6},{3,7},{4,8},{5,9},{6,10},{7,11},{16,20},{17,21},... | collective-permute-start | bytes 786440 | tf_op jit(solution)/shard_map/ppermute | solution.py:140
  210.1 1.9 fusion.62
  212.0 5.2 %collective-permute-start.24 = (bf16[128,1024]{1,0:T(8,128)(2,1)}, bf16[128,1024]{1,0:T(8,128)(2,1)S(1)}, u32[]{:S(2)}, u32[]{:S(2)}) collective-permute-start(bf16[128,1024]{1,0:T(8,128)(2,1)} %get-tuple-element.41), channel_id=1, source_target_pairs={{0,4},{1,5},{2,6},{3,7},{4,8},{5,9},{6,10},{7,11},{8,12},{9,13},{1... | collective-permute-start | bytes 786440 | tf_op jit(solution)/shard_map/ppermute | solution.py:140
  217.2 1.3 collective-permute-start.27
  218.5 0.9 fusion.56
  219.4 5.2 %collective-permute-start.31 = (bf16[128,1024]{1,0:T(8,128)(2,1)}, bf16[128,1024]{1,0:T(8,128)(2,1)S(1)}, u32[]{:S(2)}, u32[]{:S(2)}) collective-permute-start(bf16[128,1024]{1,0:T(8,128)(2,1)} %get-tuple-element.47), channel_id=1, source_target_pairs={{0,4},{1,5},{2,6},{3,7},{4,8},{5,9},{6,10},{7,11},{8,12},{9,13},{1... | collective-permute-start | bytes 786440 | tf_op jit(solution)/shard_map/ppermute | solution.py:140
  224.6 1.3 collective-permute-start.34
  225.9 0.7 collective-permute-done.27
  226.6 1.1 fusion.65
  227.6 1.1 collective-permute-done.31
  228.7 4.1 %collective-permute-done.34 = bf16[128,1024]{1,0:T(8,128)(2,1)S(1)} collective-permute-done((bf16[128,1024]{1,0:T(8,128)(2,1)S(1)}, bf16[128,1024]{1,0:T(8,128)(2,1)S(1)}, u32[]{:S(2)}, u32[]{:S(2)}) %collective-permute-start.34) | collective-permute-done | bytes 262176 | tf_op jit(solution)/shard_map/ppermute | solution.py:141
  233.0 0.8 pad_maximum_fusion
  (96 shorter events, 8.8 us)
Async XLA Ops:
  0.0 22.6 %collective-permute-start = (bf16[128,2048]{1,0:T(8,128)(2,1)}, bf16[128,2048]{1,0:T(8,128)(2,1)S(1)}, u32[]{:S(2)}, u32[]{:S(2)}) collective-permute-start(bf16[128,2048]{1,0:T(8,128)(2,1)} %param.5), channel_id=1, source_target_pairs={{0,4},{1,5},{2,6},{3,7},{4,8},{5,9},{6,10},{7,11},{8,12},{9,13},{1... | collective-permute-start | bytes 1572872 | tf_op jit(solution)/shard_map/ppermute | solution.py:70
  5.0 32.0 %collective-permute-start.7 = (bf16[128,2048]{1,0:T(8,128)(2,1)}, bf16[128,2048]{1,0:T(8,128)(2,1)S(1)}, u32[]{:S(2)}, u32[]{:S(2)}) collective-permute-start(bf16[128,2048]{1,0:T(8,128)(2,1)} %param.5), channel_id=1, source_target_pairs={{4,0},{5,1},{6,2},{7,3},{8,4},{9,5},{10,6},{11,7},{12,8},{13,9},{1... | collective-permute-start | bytes 1572872 | tf_op jit(solution)/shard_map/ppermute | solution.py:71
  6.3 69.4 %collective-permute-start.6 = (bf16[128,2048]{1,0:T(8,128)(2,1)}, bf16[128,2048]{1,0:T(8,128)(2,1)S(1)}, u32[]{:S(2)}, u32[]{:S(2)}) collective-permute-start(bf16[128,2048]{1,0:T(8,128)(2,1)} %param.5), channel_id=1, source_target_pairs={{0,2},{1,3},{2,0},{3,1},{4,6},{5,7},{6,4},{7,5},{8,10},{9,11},{10,... | collective-permute-start | bytes 1572872 | tf_op jit(solution)/shard_map/ppermute | solution.py:68
  8.7 1.2 collective-permute-start.13
  9.9 10.3 %collective-permute-start.14 = (s32[2,16,128]{2,1,0:T(8,128)S(1)}, s32[2,16,128]{2,1,0:T(8,128)S(1)}, u32[]{:S(2)}, u32[]{:S(2)}) collective-permute-start(s32[2,16,128]{2,1,0:T(8,128)S(1)} %pad_add_fusion.2), channel_id=1, source_target_pairs={{0,2},{1,3},{2,0},{3,1},{4,6},{5,7},{6,4},{7,5},{8,10},{9,11},{10,... | collective-permute-start | bytes 49160 | tf_op jit(solution)/shard_map/ppermute | solution.py:28
  20.3 4.3 %collective-permute-start.15 = (s32[4,16,128]{2,1,0:T(8,128)S(1)}, s32[4,16,128]{2,1,0:T(8,128)S(1)}, u32[]{:S(2)}, u32[]{:S(2)}) collective-permute-start(s32[4,16,128]{2,1,0:T(8,128)S(1)} %pad_add_fusion.1), channel_id=1, source_target_pairs={{0,4},{1,5},{2,6},{3,7},{4,0},{5,1},{6,2},{7,3},{8,12},{9,13},{10,... | collective-permute-start | bytes 98312 | tf_op jit(solution)/shard_map/ppermute | solution.py:28
  22.6 15.7 %collective-permute-start.1 = (bf16[128,2048]{1,0:T(8,128)(2,1)S(1)}, bf16[128,2048]{1,0:T(8,128)(2,1)S(1)}, u32[]{:S(2)}, u32[]{:S(2)}) collective-permute-start(bf16[128,2048]{1,0:T(8,128)(2,1)S(1)} %collective-permute-done), channel_id=1, source_target_pairs={{0,4},{1,5},{2,6},{3,7},{4,8},{5,9},{6,10},{7,11},{8,12},{9,13},{1... | collective-permute-start | bytes 1572872 | tf_op jit(solution)/shard_map/ppermute | solution.py:70
  24.6 11.4 %collective-permute-start.16 = (s32[8,16,128]{2,1,0:T(8,128)S(1)}, s32[8,16,128]{2,1,0:T(8,128)S(1)}, u32[]{:S(2)}, u32[]{:S(2)}) collective-permute-start(s32[8,16,128]{2,1,0:T(8,128)S(1)} %pad_add_fusion), channel_id=1, source_target_pairs={{0,8},{1,9},{2,10},{3,11},{4,12},{5,13},{6,14},{7,15},{8,0},{9,1},... | collective-permute-start | bytes 196616 | tf_op jit(solution)/shard_map/ppermute | solution.py:28
  37.0 14.3 %collective-permute-start.9 = (bf16[128,2048]{1,0:T(8,128)(2,1)S(1)}, bf16[128,2048]{1,0:T(8,128)(2,1)S(1)}, u32[]{:S(2)}, u32[]{:S(2)}) collective-permute-start(bf16[128,2048]{1,0:T(8,128)(2,1)S(1)} %collective-permute-done.7), channel_id=1, source_target_pairs={{4,0},{5,1},{6,2},{7,3},{8,4},{9,5},{10,6},{11,7},{12,8},{13,9},{1... | collective-permute-start | bytes 1572872 | tf_op jit(solution)/shard_map/ppermute | solution.py:71
  38.3 14.3 %collective-permute-start.2 = (bf16[128,2048]{1,0:T(8,128)(2,1)S(1)}, bf16[128,2048]{1,0:T(8,128)(2,1)S(1)}, u32[]{:S(2)}, u32[]{:S(2)}) collective-permute-start(bf16[128,2048]{1,0:T(8,128)(2,1)S(1)} %collective-permute-done.1), channel_id=1, source_target_pairs={{0,4},{1,5},{2,6},{3,7},{4,8},{5,9},{6,10},{7,11},{8,12},{9,13},{1... | collective-permute-start | bytes 1572872 | tf_op jit(solution)/shard_map/ppermute | solution.py:70
  46.6 9.6 %copy-start.1 = (bf16[128,2048]{1,0:T(8,128)(2,1)S(1)}, bf16[128,2048]{1,0:T(8,128)(2,1)}, u32[]{:S(2)}) copy-start(bf16[128,2048]{1,0:T(8,128)(2,1)} %param.5) | copy-start | bytes 1572868
  46.7 32.4 %collective-permute-start.5 = (bf16[128,2048]{1,0:T(8,128)(2,1)S(1)}, bf16[128,2048]{1,0:T(8,128)(2,1)S(1)}, u32[]{:S(2)}, u32[]{:S(2)}) collective-permute-start(bf16[128,2048]{1,0:T(8,128)(2,1)S(1)} %collective-permute-done), channel_id=1, source_target_pairs={{4,6},{5,7},{6,4},{7,5},{8,10},{9,11},{10,8},{11,9},{12,14},{13,15... | collective-permute-start | bytes 1572872 | tf_op jit(solution)/shard_map/ppermute | solution.py:77
  47.5 37.1 %collective-permute-start.8 = (bf16[128,2048]{1,0:T(8,128)(2,1)S(1)}, bf16[128,2048]{1,0:T(8,128)(2,1)S(1)}, u32[]{:S(2)}, u32[]{:S(2)}) collective-permute-start(bf16[128,2048]{1,0:T(8,128)(2,1)S(1)} %collective-permute-done.7), channel_id=1, source_target_pairs={{0,2},{1,3},{2,0},{3,1},{4,6},{5,7},{6,4},{7,5},{8,10},{9,11},{10,... | collective-permute-start | bytes 1572872 | tf_op jit(solution)/shard_map/ppermute | solution.py:79
  51.3 12.7 %collective-permute-start.11 = (bf16[128,2048]{1,0:T(8,128)(2,1)S(1)}, bf16[128,2048]{1,0:T(8,128)(2,1)S(1)}, u32[]{:S(2)}, u32[]{:S(2)}) collective-permute-start(bf16[128,2048]{1,0:T(8,128)(2,1)S(1)} %collective-permute-done.9), channel_id=1, source_target_pairs={{4,0},{5,1},{6,2},{7,3},{8,4},{9,5},{10,6},{11,7},{12,8},{13,9},{1... | collective-permute-start | bytes 1572872 | tf_op jit(solution)/shard_map/ppermute | solution.py:71
  52.6 32.0 %collective-permute-start.10 = (bf16[128,2048]{1,0:T(8,128)(2,1)S(1)}, bf16[128,2048]{1,0:T(8,128)(2,1)S(1)}, u32[]{:S(2)}, u32[]{:S(2)}) collective-permute-start(bf16[128,2048]{1,0:T(8,128)(2,1)S(1)} %collective-permute-done.9), channel_id=1, source_target_pairs={{0,2},{1,3},{2,0},{3,1},{4,6},{5,7},{6,4},{7,5},{16,18},{17,19},{1... | collective-permute-start | bytes 1572872 | tf_op jit(solution)/shard_map/ppermute | solution.py:79
  64.0 20.7 %collective-permute-start.4 = (bf16[128,2048]{1,0:T(8,128)(2,1)S(1)}, bf16[128,2048]{1,0:T(8,128)(2,1)S(1)}, u32[]{:S(2)}, u32[]{:S(2)}) collective-permute-start(bf16[128,2048]{1,0:T(8,128)(2,1)S(1)} %collective-permute-done.1), channel_id=1, source_target_pairs={{8,10},{9,11},{10,8},{11,9},{12,14},{13,15},{14,12},{15,13},{24,26... | collective-permute-start | bytes 1572872 | tf_op jit(solution)/shard_map/ppermute | solution.py:77
  64.7 5.9 %slice-start = ((s8[12582912]{0:T(1024)(128)(4,1)}), s8[4194304]{0:T(1024)(128)(4,1)S(1)}, s32[]{:S(2)}) async-start(s8[12582912]{0:T(1024)(128)(4,1)} %bitcast.133), calls=%async_computation | async-start | bytes 8388608
  64.9 5.7 %slice-start.1 = ((s8[12582912]{0:T(1024)(128)(4,1)}), s8[4194304]{0:T(1024)(128)(4,1)S(1)}, s32[]{:S(2)}) async-start(s8[12582912]{0:T(1024)(128)(4,1)} %bitcast.133), calls=%async_computation.1 | async-start | bytes 8388608
  64.9 6.4 %slice-start.2 = ((s8[12582912]{0:T(1024)(128)(4,1)}), s8[4194304]{0:T(1024)(128)(4,1)S(1)}, s32[]{:S(2)}) async-start(s8[12582912]{0:T(1024)(128)(4,1)} %bitcast.133), calls=%async_computation.2 | async-start | bytes 8388608
  64.9 15.0 %slice-start.3 = ((s8[6291456]{0:T(1024)(128)(4,1)}), s8[4194304]{0:T(1024)(128)(4,1)S(1)}, s32[]{:S(2)}) async-start(s8[6291456]{0:T(1024)(128)(4,1)} %bitcast.135), calls=%async_computation.3 | async-start | bytes 8388608
  71.3 8.7 %slice-start.4 = ((s8[6291456]{0:T(1024)(128)(4,1)}), s8[2097152]{0:T(1024)(128)(4,1)S(1)}, s32[]{:S(2)}) async-start(s8[6291456]{0:T(1024)(128)(4,1)} %bitcast.135), calls=%async_computation.4 | async-start | bytes 4194304
  75.6 11.1 %collective-permute-start.12 = (bf16[128,2048]{1,0:T(8,128)(2,1)S(1)}, bf16[128,2048]{1,0:T(8,128)(2,1)S(1)}, u32[]{:S(2)}, u32[]{:S(2)}) collective-permute-start(bf16[128,2048]{1,0:T(8,128)(2,1)S(1)} %collective-permute-done.11), channel_id=1, source_target_pairs={{0,2},{1,3},{2,0},{3,1},{16,18},{17,19},{18,16},{19,17}} | collective-permute-start | bytes 1572872 | tf_op jit(solution)/shard_map/ppermute | solution.py:79
  79.1 7.6 %collective-permute-start.3 = (bf16[128,2048]{1,0:T(8,128)(2,1)S(1)}, bf16[128,2048]{1,0:T(8,128)(2,1)S(1)}, u32[]{:S(2)}, u32[]{:S(2)}) collective-permute-start(bf16[128,2048]{1,0:T(8,128)(2,1)S(1)} %collective-permute-done.2), channel_id=1, source_target_pairs={{12,14},{13,15},{14,12},{15,13},{28,30},{29,31},{30,28},{31,29}} | collective-permute-start | bytes 1572872 | tf_op jit(solution)/shard_map/ppermute | solution.py:77
  87.2 4.2 %collective-permute-start.17 = (bf16[512,2048]{1,0:T(8,128)(2,1)S(1)}, bf16[512,2048]{1,0:T(8,128)(2,1)S(1)}, u32[]{:S(2)}, u32[]{:S(2)}) collective-permute-start(bf16[512,2048]{1,0:T(8,128)(2,1)S(1)} %constant_dynamic-slice_fusion), channel_id=1, source_target_pairs={{0,1},{1,0},{2,3},{3,2},{4,5},{5,4},{6,7},{7,6},{8,9},{9,8},{10,11... | collective-permute-start | bytes 6291464 | tf_op jit(solution)/shard_map/ppermute | solution.py:109
  87.3 30.0 %collective-permute-start.18 = (bf16[512,2048]{1,0:T(8,128)(2,1)S(1)}, bf16[512,2048]{1,0:T(8,128)(2,1)S(1)}, u32[]{:S(2)}, u32[]{:S(2)}) collective-permute-start(bf16[512,2048]{1,0:T(8,128)(2,1)S(1)} %constant_dynamic-slice_fusion.1), channel_id=1, source_target_pairs={{0,1},{1,0},{2,3},{3,2},{4,5},{5,4},{6,7},{7,6},{8,9},{9,8},{10,11... | collective-permute-start | bytes 6291464 | tf_op jit(solution)/shard_map/ppermute | solution.py:89
  103.1 11.7 %collective-permute-start.19 = (bf16[512,2048]{1,0:T(8,128)(2,1)S(1)}, bf16[512,2048]{1,0:T(8,128)(2,1)S(1)}, u32[]{:S(2)}, u32[]{:S(2)}) collective-permute-start(bf16[512,2048]{1,0:T(8,128)(2,1)S(1)} %convolution_convert_fusion.2), channel_id=1, source_target_pairs={{0,1},{1,0},{2,3},{3,2},{4,5},{5,4},{6,7},{7,6},{8,9},{9,8},{10,11... | collective-permute-start | bytes 6291464 | tf_op jit(solution)/shard_map/ppermute | solution.py:111
  115.7 25.5 %collective-permute-start.20 = (bf16[512,1024]{1,0:T(8,128)(2,1)S(1)}, bf16[512,1024]{1,0:T(8,128)(2,1)S(1)}, u32[]{:S(2)}, u32[]{:S(2)}) collective-permute-start(bf16[512,1024]{1,0:T(8,128)(2,1)S(1)} %get-tuple-element.39), channel_id=1, source_target_pairs={{0,2},{1,3},{2,0},{3,1},{4,6},{5,7},{6,4},{7,5},{8,10},{9,11},{10,... | collective-permute-start | bytes 3145736 | tf_op jit(solution)/shard_map/ppermute | solution.py:115
  154.0 26.5 %collective-permute-start.21 = (bf16[512,2048]{1,0:T(8,128)(2,1)}, bf16[512,2048]{1,0:T(8,128)(2,1)}, u32[]{:S(2)}, u32[]{:S(2)}) collective-permute-start(bf16[512,2048]{1,0:T(8,128)(2,1)} %convolution_convert_fusion), channel_id=1, source_target_pairs={{0,1},{1,0},{2,3},{3,2},{4,5},{5,4},{6,7},{7,6},{8,9},{9,8},{10,11... | collective-permute-start | bytes 6291464 | tf_op jit(solution)/shard_map/ppermute | solution.py:119
  154.0 25.6 %collective-permute-start.28 = (bf16[512,1024]{1,0:T(8,128)(2,1)S(1)}, bf16[512,1024]{1,0:T(8,128)(2,1)S(1)}, u32[]{:S(2)}, u32[]{:S(2)}) collective-permute-start(bf16[512,1024]{1,0:T(8,128)(2,1)S(1)} %get-tuple-element.40), channel_id=1, source_target_pairs={{0,2},{1,3},{2,0},{3,1},{4,6},{5,7},{6,4},{7,5},{8,10},{9,11},{10,... | collective-permute-start | bytes 3145736 | tf_op jit(solution)/shard_map/ppermute | solution.py:115
  179.6 1.0 copy-start
  184.5 8.0 %collective-permute-start.22 = (bf16[128,1024]{1,0:T(8,128)(2,1)S(1)}, bf16[128,1024]{1,0:T(8,128)(2,1)}, u32[]{:S(2)}, u32[]{:S(2)}) collective-permute-start(bf16[128,1024]{1,0:T(8,128)(2,1)S(1)} %get-tuple-element.45), channel_id=1, source_target_pairs={{0,4},{1,5},{2,6},{3,7},{16,20},{17,21},{18,22},{19,23}} | collective-permute-start | bytes 786440 | tf_op jit(solution)/shard_map/ppermute | solution.py:140
  186.5 6.0 %collective-permute-start.25 = (bf16[128,1024]{1,0:T(8,128)(2,1)S(1)}, bf16[128,1024]{1,0:T(8,128)(2,1)}, u32[]{:S(2)}, u32[]{:S(2)}) collective-permute-start(bf16[128,1024]{1,0:T(8,128)(2,1)S(1)} %get-tuple-element.46), channel_id=1, source_target_pairs={{12,8},{13,9},{14,10},{15,11},{28,24},{29,25},{30,26},{31,27}} | collective-permute-start | bytes 786440 | tf_op jit(solution)/shard_map/ppermute | solution.py:141
  187.9 12.4 %collective-permute-start.29 = (bf16[128,1024]{1,0:T(8,128)(2,1)S(1)}, bf16[128,1024]{1,0:T(8,128)(2,1)S(1)}, u32[]{:S(2)}, u32[]{:S(2)}) collective-permute-start(bf16[128,1024]{1,0:T(8,128)(2,1)S(1)} %get-tuple-element.51), channel_id=1, source_target_pairs={{0,4},{1,5},{2,6},{3,7},{16,20},{17,21},{18,22},{19,23}} | collective-permute-start | bytes 786440 | tf_op jit(solution)/shard_map/ppermute | solution.py:140
  189.2 11.1 %collective-permute-start.32 = (bf16[128,1024]{1,0:T(8,128)(2,1)S(1)}, bf16[128,1024]{1,0:T(8,128)(2,1)}, u32[]{:S(2)}, u32[]{:S(2)}) collective-permute-start(bf16[128,1024]{1,0:T(8,128)(2,1)S(1)} %get-tuple-element.52), channel_id=1, source_target_pairs={{12,8},{13,9},{14,10},{15,11},{28,24},{29,25},{30,26},{31,27}} | collective-permute-start | bytes 786440 | tf_op jit(solution)/shard_map/ppermute | solution.py:141
  194.4 15.7 %collective-permute-start.23 = (bf16[128,1024]{1,0:T(8,128)(2,1)}, bf16[128,1024]{1,0:T(8,128)(2,1)S(1)}, u32[]{:S(2)}, u32[]{:S(2)}) collective-permute-start(bf16[128,1024]{1,0:T(8,128)(2,1)} %get-tuple-element.43), channel_id=1, source_target_pairs={{0,4},{1,5},{2,6},{3,7},{4,8},{5,9},{6,10},{7,11},{16,20},{17,21},... | collective-permute-start | bytes 786440 | tf_op jit(solution)/shard_map/ppermute | solution.py:140
  198.9 11.2 %collective-permute-start.26 = (bf16[128,1024]{1,0:T(8,128)(2,1)S(1)}, bf16[128,1024]{1,0:T(8,128)(2,1)}, u32[]{:S(2)}, u32[]{:S(2)}) collective-permute-start(bf16[128,1024]{1,0:T(8,128)(2,1)S(1)} %get-tuple-element.44), channel_id=1, source_target_pairs={{8,4},{9,5},{10,6},{11,7},{12,8},{13,9},{14,10},{15,11},{24,20},{2... | collective-permute-start | bytes 786440 | tf_op jit(solution)/shard_map/ppermute | solution.py:141
  202.2 16.3 %collective-permute-start.30 = (bf16[128,1024]{1,0:T(8,128)(2,1)}, bf16[128,1024]{1,0:T(8,128)(2,1)S(1)}, u32[]{:S(2)}, u32[]{:S(2)}) collective-permute-start(bf16[128,1024]{1,0:T(8,128)(2,1)} %get-tuple-element.49), channel_id=1, source_target_pairs={{0,4},{1,5},{2,6},{3,7},{4,8},{5,9},{6,10},{7,11},{16,20},{17,21},... | collective-permute-start | bytes 786440 | tf_op jit(solution)/shard_map/ppermute | solution.py:140
  209.4 9.0 %collective-permute-start.33 = (bf16[128,1024]{1,0:T(8,128)(2,1)S(1)}, bf16[128,1024]{1,0:T(8,128)(2,1)S(1)}, u32[]{:S(2)}, u32[]{:S(2)}) collective-permute-start(bf16[128,1024]{1,0:T(8,128)(2,1)S(1)} %get-tuple-element.50), channel_id=1, source_target_pairs={{8,4},{9,5},{10,6},{11,7},{12,8},{13,9},{14,10},{15,11},{24,20},{2... | collective-permute-start | bytes 786440 | tf_op jit(solution)/shard_map/ppermute | solution.py:141
  212.0 13.9 %collective-permute-start.24 = (bf16[128,1024]{1,0:T(8,128)(2,1)}, bf16[128,1024]{1,0:T(8,128)(2,1)S(1)}, u32[]{:S(2)}, u32[]{:S(2)}) collective-permute-start(bf16[128,1024]{1,0:T(8,128)(2,1)} %get-tuple-element.41), channel_id=1, source_target_pairs={{0,4},{1,5},{2,6},{3,7},{4,8},{5,9},{6,10},{7,11},{8,12},{9,13},{1... | collective-permute-start | bytes 786440 | tf_op jit(solution)/shard_map/ppermute | solution.py:140
  217.2 9.4 %collective-permute-start.27 = (bf16[128,1024]{1,0:T(8,128)(2,1)S(1)}, bf16[128,1024]{1,0:T(8,128)(2,1)}, u32[]{:S(2)}, u32[]{:S(2)}) collective-permute-start(bf16[128,1024]{1,0:T(8,128)(2,1)S(1)} %get-tuple-element.42), channel_id=1, source_target_pairs={{4,0},{5,1},{6,2},{7,3},{8,4},{9,5},{10,6},{11,7},{12,8},{13,9},{1... | collective-permute-start | bytes 786440 | tf_op jit(solution)/shard_map/ppermute | solution.py:141
  219.4 9.3 %collective-permute-start.31 = (bf16[128,1024]{1,0:T(8,128)(2,1)}, bf16[128,1024]{1,0:T(8,128)(2,1)S(1)}, u32[]{:S(2)}, u32[]{:S(2)}) collective-permute-start(bf16[128,1024]{1,0:T(8,128)(2,1)} %get-tuple-element.47), channel_id=1, source_target_pairs={{0,4},{1,5},{2,6},{3,7},{4,8},{5,9},{6,10},{7,11},{8,12},{9,13},{1... | collective-permute-start | bytes 786440 | tf_op jit(solution)/shard_map/ppermute | solution.py:140
  224.6 8.3 %collective-permute-start.34 = (bf16[128,1024]{1,0:T(8,128)(2,1)S(1)}, bf16[128,1024]{1,0:T(8,128)(2,1)S(1)}, u32[]{:S(2)}, u32[]{:S(2)}) collective-permute-start(bf16[128,1024]{1,0:T(8,128)(2,1)S(1)} %get-tuple-element.48), channel_id=1, source_target_pairs={{4,0},{5,1},{6,2},{7,3},{8,4},{9,5},{10,6},{11,7},{12,8},{13,9},{1... | collective-permute-start | bytes 786440 | tf_op jit(solution)/shard_map/ppermute | solution.py:141
